TPU v7x, 128 devices: a whole 4x4x4 slice. The times are simulated.
128 devices in a mesh: op: 16 (over z, x), sec: 8 (over y, core).
Axes of the slice: x: 4, y: 4, z: 4, core: 2. Of those that a mesh axis runs over, the one named last changes fastest.
Arguments:
- psi: bfloat16 [256, 128, 256], P('sec', 'op'), may hold values from -6 to 6
- left_env: bfloat16 [128, 256, 128, 128], P('op', 'sec'), may hold values from -0.5 to 0.5
- right_env: bfloat16 [128, 8, 256, 256], P('op', 'sec'), may hold values from -0.375 to 0.375
- source: int32 [128, 256], P('op', 'sec'), may hold values from 0 to 255, as said below
- coupling: int32 [128, 256], P('op', 'sec'), may hold values from 0 to 3
Outputs:
- sigma: bfloat16 [256, 128, 256], P('sec', 'op')
- renorm: float32 [128, 8, 256, 256], P(('op', 'sec'))
Inputs may be any that keep to these rules, and one draw needn't show every extreme that they name: source[k, s] lies in the same aligned block of 32 sectors as s.
All inputs are finite; a program needn't handle non-finite values.
Results may differ from a plain program's by a relative error of at most 0.011.
Values may be sent and summed in bfloat16 or wider, within the bound.
A program may use at most 128 MiB of HBM per device.

v0:
```python
import jax
import jax.numpy as jnp
from jax import lax
from jax.sharding import PartitionSpec as P

COEFS = (1.0, -0.5773503, 0.8164966, -0.7071068)


def body(psi, left_env, right_env, source, coupling):
    kdev, sdev = source.shape
    rows = psi.shape[1]
    full = lax.all_gather(psi, "op", axis=1, tiled=True)
    block = full.shape[1]
    local_src = source % sdev
    picked = full[local_src]
    mixed = jnp.einsum(
        "ksab,ksbm->ksam", left_env, picked, preferred_element_type=jnp.float32
    ).astype(jnp.bfloat16)
    image = jnp.einsum("ksam,kmn->ksan", mixed, right_env[:, 0], preferred_element_type=jnp.float32)
    coef = jnp.zeros(coupling.shape, jnp.float32)
    for level in range(4):
        coef = coef + jnp.where(coupling == level, COEFS[level], 0.0)
    kops = kdev * lax.axis_size("op")
    partial_sigma = jnp.einsum("ks,ksan->san", coef, image) * kops ** (-0.5)
    group_renorm = jnp.einsum("sbm,ksbn->kmn", full, mixed, preferred_element_type=jnp.float32) * (
        sdev * block
    ) ** (-0.5)
    renorm = lax.all_to_all(group_renorm[:, None], "sec", split_axis=0, concat_axis=1, tiled=True)
    summed = lax.psum(partial_sigma, "op")
    sigma = lax.dynamic_slice_in_dim(summed, lax.axis_index("op") * rows, rows, 1)
    return (sigma.astype(jnp.bfloat16), renorm)


def solution(mesh):
    placed = (
        P("sec", "op", None),
        P("op", "sec", None, None),
        P("op", "sec", None, None),
        P("op", "sec"),
        P("op", "sec"),
    )
    return jax.shard_map(
        body,
        mesh=mesh,
        in_specs=placed,
        out_specs=(P("sec", "op", None), P(("op", "sec"), None, None, None)),
        check_vma=False,
    )
```

profile of v0, /device:TPU:0, one launch (start us, length us, event | category | flops | bytes accessed | tf_op | source)
XLA Modules:
  0.0 254.2 jit_solution(6759004748961544293)
XLA Ops:
  7.2 0.0 copy-start
  7.2 0.0 all-gather.2.cloned.1.call-start
  7.2 0.7 all-gather.2.cloned.1.call-update
  7.9 0.7 compare_select_fusion
  8.6 0.1 reshape.9
  8.7 0.7 add_bitcast_fusion
  9.4 0.1 copy.14
  9.5 50.9 %all-gather.2.cloned.1.call-done = bf16[32,128,256]{2,1,0:T(8,128)(2,1)} async-done(((bf16[32,8,256]{2,1,0:T(8,128)(2,1)}), bf16[32,128,256]{2,1,0:T(8,128)(2,1)}) %all-gather.2.cloned.1.call-update) | async-done | bytes 2097168 | tf_op jit(solution)/shard_map/all_gather | solution.py:12
  60.4 11.3 %gather_fusion = bf16[256,128,256]{2,1,0:T(8,128)(2,1)} fusion(bf16[32,128,256]{2,1,0:T(8,128)(2,1)} %all-gather.2.cloned.1.call-done, s32[1024]{0:T(1024)S(1)} %pad_clamp_fusion), kind=kCustom, calls=%fused_computation | custom fusion | bytes 33555456 | tf_op jit(solution)/shard_map/gather | solution.py:15
  71.7 21.1 %convolution_convert_fusion = bf16[8,32,256,128]{3,2,1,0:T(8,128)(2,1)} fusion(bf16[8,32,128,256]{3,2,1,0:T(8,128)(2,1)} %bitcast.38, bf16[8,32,128,128]{3,2,1,0:T(8,128)(2,1)} %param.6), kind=kOutput, calls=%fused_computation.7 | convolution fusion | flops 2155872256 | bytes 41943040 | tf_op jit(solution)/shard_map/ksab,ksbm->ksam/dot_general | solution.py:16
  92.8 0.0 copy-done
  92.8 15.1 %fusion.4 = bf16[8,32,128,256]{3,2,1,0:T(8,128)(2,1)} fusion(bf16[8,32,256,128]{3,2,1,0:T(8,128)(2,1)} %convolution_convert_fusion, bf16[8,1,256,256]{3,2,1,0:T(8,128)(2,1)S(1)} %copy-done), kind=kOutput, calls=%fused_computation.5 | convolution fusion | flops 4294967296 | bytes 34603008 | tf_op jit(solution)/shard_map/ksam,kmn->ksan/dot_general | solution.py:19
  107.9 16.4 %fusion = f32[32,1,128,256]{3,1,2,0:T(1,128)S(1)} fusion(bf16[8,32,1,1]{0,2,3,1:T(2,128)(2,1)S(1)} %copy.14, bf16[8,32,128,256]{3,2,1,0:T(8,128)(2,1)} %fusion.4), kind=kOutput, calls=%fused_computation.1 | convolution fusion | flops 16777216 | bytes 20972032 | tf_op jit(solution)/shard_map/ks,ksan->san/dot_general | solution.py:24
  124.3 0.0 copy-start.2
  124.3 2.6 %bitcast_multiply_fusion = f32[32,128,256]{2,1,0:T(8,128)} fusion(f32[32,1,128,256]{3,1,2,0:T(1,128)S(1)} %fusion), kind=kLoop, calls=%fused_computation.8 | loop fusion | flops 1048576 | bytes 8388608 | tf_op jit(solution)/shard_map/mul | solution.py:24
  127.0 0.0 copy-done.2
  127.0 0.0 copy-start.1
  127.0 9.2 %fusion.6 = f32[8,1,256,256]{2,3,1,0:T(8,128)} fusion(bf16[32,128,256]{2,1,0:T(8,128)(2,1)S(1)} %copy-done.2, bf16[8,32,256,128]{3,2,1,0:T(8,128)(2,1)} %convolution_convert_fusion), kind=kOutput, calls=%fused_computation.10 | convolution fusion | flops 4295491584 | bytes 20971520 | tf_op jit(solution)/shard_map/sbm,ksbn->kmn/dot_general | solution.py:25
  136.2 4.3 %all-to-all-start = ((f32[8,1,256,256]{2,3,1,0:T(8,128)}), f32[8,1,256,256]{2,3,1,0:T(8,128)S(1)}, u32[]{:S(2)}, u32[]{:S(2)}) async-start(f32[8,1,256,256]{2,3,1,0:T(8,128)} %fusion.6), calls=%async_computation | async-start | bytes 4194304 | tf_op jit(solution)/shard_map/all_to_all | solution.py:28
  140.5 103.5 %all-reduce.1 = bf16[32,128,256]{2,1,0:T(8,128)(2,1)} all-reduce(f32[32,128,256]{2,1,0:T(8,128)} %bitcast_multiply_fusion), channel_id=1, replica_groups=mesh['op'=16,'sec'=8] {'op'}, use_global_device_ids=true, to_apply=%region_0.1 | all-reduce | flops 1048576 | bytes 6291456 | tf_op jit(solution)/shard_map/psum | solution.py:29
  243.9 1.6 dynamic-slice_convert_fusion
  245.5 0.0 all-to-all-done
  245.5 1.8 copy.11
  247.3 0.0 copy-done.1
  (1 shorter events, 0.0 us)
Async XLA Ops:
  7.2 85.7 %copy-start = (bf16[8,1,256,256]{3,2,1,0:T(8,128)(2,1)S(1)}, bf16[8,1,256,256]{3,2,1,0:T(8,128)(2,1)}, u32[]{:S(2)}) copy-start(bf16[8,1,256,256]{3,2,1,0:T(8,128)(2,1)} %param.7) | copy-start | bytes 3145732
  7.2 53.2 %all-gather.2.cloned.1.call-start = ((), (), s32[]{:S(2)}) async-start(), calls=%async_computation.1 | async-start | bytes 2228224 | tf_op jit(solution)/shard_map/all_gather | solution.py:12
  124.3 2.6 %copy-start.2 = (bf16[32,128,256]{2,1,0:T(8,128)(2,1)S(1)}, bf16[32,128,256]{2,1,0:T(8,128)(2,1)}, u32[]{:S(2)}) copy-start(bf16[32,128,256]{2,1,0:T(8,128)(2,1)} %all-gather.2.cloned.1.call-done) | copy-start | bytes 6291460
  127.0 120.4 %copy-start.1 = (bf16[8,1,256,256]{3,2,1,0:T(8,128)(2,1)S(1)}, bf16[8,1,256,256]{3,2,1,0:T(8,128)(2,1)}, u32[]{:S(2)}) copy-start(bf16[8,1,256,256]{3,2,1,0:T(8,128)(2,1)} %param.7) | copy-start | bytes 3145732
  136.2 109.3 %all-to-all-start = ((f32[8,1,256,256]{2,3,1,0:T(8,128)}), f32[8,1,256,256]{2,3,1,0:T(8,128)S(1)}, u32[]{:S(2)}, u32[]{:S(2)}) async-start(f32[8,1,256,256]{2,3,1,0:T(8,128)} %fusion.6), calls=%async_computation | async-start | bytes 4194304 | tf_op jit(solution)/shard_map/all_to_all | solution.py:28
Sparse Core Ops, SparseCore 0:
  10.1 50.2 all-gather.1
where the time goes:
time: 255 us; the launch traced here: 254 us
  blocking collectives  103 us (40%)
  matrix products  61.8 us (24%)
  waiting for transfers between devices  51.6 us (20%)
  local copies, waits for them, and re-layouts  14.9 us (6%)
  between operations  14.1 us (6%)
  starting transfers between devices  4.34 us (2%)
  other arithmetic  4.02 us (2%)
    psum x1, blocking collectives, body(): summed = lax.psum(partial_sigma, 'op')  103 us
    all_gather x1, waiting for transfers between devices, body(): full = lax.all_gather(psi, 'op', axis=1, tiled=True)  50.9 us
    dot_general x1, matrix products, body(): jnp.einsum('ksab,ksbm->ksam', left_env, picked, preferred_element_type=jn...  21.1 us
    dot_general x1, matrix products, body(): partial_sigma = jnp.einsum('ks,ksan->san', coef, image) * kops ** (-0.5)  16.4 us
    dot_general x1, matrix products, body(): jnp.einsum('ksam,kmn->ksan', mixed, right_env[:, 0], preferred_element_ty...  15.1 us
    gather x1, local copies, waits for them, and re-layouts, body(): picked = full[local_src]  11.3 us
    dot_general x1, matrix products, body(): jnp.einsum('sbm,ksbn->kmn', full, mixed, preferred_element_type=jnp.float32)  9.21 us
  transfers between devices with their start and end apart: 2, of which 1 were waited for; matrix products, arithmetic and copies ran while one was open for 1% of the time, Pallas kernels for 0%

commit v1 on v0

v1 whole, which is shorter than its diff:
```python
import functools

import jax
import jax.numpy as jnp
from jax import lax
from jax.experimental import pallas as pl
from jax.experimental.pallas import tpu as pltpu
from jax.sharding import PartitionSpec as P

COEFS = (1.0, -0.5773503, 0.8164966, -0.7071068)
MESH = pl.DeviceIdType.MESH
F32 = jnp.float32
BF16 = jnp.bfloat16
CHUNKS = 4


def turn(a, step):
    return lax.rem(a + step, 4)


def kernel(
    psi_ref, left_ref, right_ref, src_ref, cpl_ref,
    sig_ref, ren_ref,
    left, scaled, right, got, full, full_t, image, zed, parts, block,
    hop1, hop2, kept, hop3, hop4, relay,
    load_sem, send_sem, gather_sem, sum_sem, swap_sem, relay_sem, far_sem, own_sem,
    acc00, acc01, acc02, acc03, acc10, acc11, acc12, acc13,
):
    acc = ((acc00, acc01, acc02, acc03), (acc10, acc11, acc12, acc13))
    op, sec = lax.axis_index("op"), lax.axis_index("sec")
    z, x = op // 4, op % 4
    y, core = sec // 2, sec % 2
    coords = ((x, z), (z, x))

    loads = [
        pltpu.make_async_copy(psi_ref.at[pl.ds(h * 128, 128)], got.at[h, op], load_sem.at[h]) for h in range(2)
    ]
    loads.append(pltpu.make_async_copy(left_ref, left, load_sem.at[2]))
    loads.append(pltpu.make_async_copy(right_ref, right, load_sem.at[3]))
    for copy in loads:
        copy.start()

    barrier = pltpu.get_barrier_semaphore()
    peers = [(z * 4 + turn(x, 1), sec), (z * 4 + turn(x, 3), sec), (turn(z, 1) * 4 + x, sec), (turn(z, 3) * 4 + x, sec)]
    peers += [(op, lax.rem(sec + i, 8)) for i in range(1, 8)]
    for peer in peers:
        pl.semaphore_signal(barrier, inc=1, device_id=peer, device_id_type=MESH)
    pl.semaphore_wait(barrier, len(peers))

    sent = []

    def place(h, p, q):
        return q * 4 + p if h == 0 else p * 4 + q

    def at(h, dp, dq):
        p, q = coords[h]
        return place(h, turn(p, dp), turn(q, dq))

    def start(src, dst, recv_sem, target):
        copy = pltpu.make_async_remote_copy(
            src_ref=src, dst_ref=dst, send_sem=send_sem.at[len(sent)], recv_sem=recv_sem,
            device_id=(target, sec), device_id_type=MESH,
        )
        copy.start()
        sent.append(copy)

    def arrived(dst, recv_sem):
        pltpu.make_async_remote_copy(
            src_ref=dst, dst_ref=dst, send_sem=send_sem.at[0], recv_sem=recv_sem,
            device_id=(op, sec), device_id_type=MESH,
        ).wait_recv()

    def piece(h, dp, dq, half):
        ref = got.at[h, at(h, dp, dq)]
        return ref if half is None else ref.at[pl.ds(half * 64, 64)]

    def pass_on(h, dp, dq, half, sp, sq):
        ref = piece(h, dp, dq, half)
        rel = (dp - sp) % 4 * 4 + (dq - sq) % 4
        start(ref, ref, gather_sem.at[h, rel, 0 if half is None else half], at(h, sp % 4, sq % 4))

    def await_piece(h, dp, dq, half):
        arrived(piece(h, dp, dq, half), gather_sem.at[h, dp * 4 + dq, 0 if half is None else half])

    for h in range(2):
        loads[h].wait()
        for sp in (1, -1):
            pass_on(h, 0, 0, None, sp, 0)
    for h in range(2):
        for sq in (1, -1):
            pass_on(h, 0, 0, None, 0, sq)

    def scale(part):
        @pl.loop(2 * part, 2 * part + 2)
        def _(k):
            @pl.loop(0, 32, unroll=8)
            def _(s):
                level = cpl_ref[k, s]
                coef = jnp.where(
                    level == 0, COEFS[0], jnp.where(level == 1, COEFS[1], jnp.where(level == 2, COEFS[2], COEFS[3]))
                )
                scaled[k, s] = (left[k, s].astype(F32) * coef).astype(BF16)

    def pair_image(h, zz, j):
        to = pl.ds(pl.multiple_of(zz * 32 + j * 16, 16), 16)

        def put(ref, first, second):
            for s in range(16):
                two = jnp.concatenate([first[s * 8 : s * 8 + 8], second[s * 8 : s * 8 + 8]], axis=0)
                ref[h * 16 + s, to, :] = two.astype(BF16)

        def rows_in(o):
            return got[h, zz * 4 + 2 * j + o]

        put(full, rows_in(0).astype(F32), rows_in(1).astype(F32))
        for k in range(8):
            unit, reg = k % 2, k // 2 % 2
            pltpu.matmul_push_rhs(right[k], reg, unit)
            for o in range(2):
                pltpu.matmul_acc_lhs(acc[unit][2 * reg + o], rows_in(o), reg if o == 0 else None)
            put(image.at[k], pltpu.matmul_pop(acc[unit][2 * reg]), pltpu.matmul_pop(acc[unit][2 * reg + 1]))

    def images(count, which):
        @pl.loop(0, count)
        def _(i):
            h, dz, other = which(i)
            j = x // 2
            pair_image(h, lax.rem(z + dz, 4), j + other * (1 - 2 * j))

    loads[2].wait()
    scale(0)
    for h in range(2):
        for dp, half, sp in ((3, 0, 1), (1, 1, -1)):
            await_piece(h, dp, 0, None)
            pass_on(h, dp, 0, half, sp, 0)
            for sq in (1, -1):
                pass_on(h, dp, 0, None, 0, sq)
    for h in range(2):
        for dq, half, sq in ((3, 0, 1), (1, 1, -1)):
            await_piece(h, 0, dq, None)
            pass_on(h, 0, dq, half, 0, sq)
    loads[3].wait()
    images(2, lambda i: (i, 0, 0))
    for h in range(2):
        await_piece(h, 2, 0, 0)
        await_piece(h, 2, 0, 1)
        for sq in (1, -1):
            pass_on(h, 2, 0, None, 0, sq)
    scale(1)
    for h in range(2):
        await_piece(h, 0, 2, 0)
        await_piece(h, 0, 2, 1)
    images(2, lambda i: (i, 0, 1))
    scale(2)
    for h in range(2):
        for dp in (3, 1):
            for dq, half, sq in ((3, 0, 1), (1, 1, -1)):
                await_piece(h, dp, dq, None)
                pass_on(h, dp, dq, half, 0, sq)
    images(4, lambda i: (i // 2, 3 + 2 * (i % 2), 0))
    for h in range(2):
        for dq, half, sq in ((3, 0, 1), (1, 1, -1)):
            await_piece(h, 2, dq, None)
            pass_on(h, 2, dq, half, 0, sq)
    scale(3)
    images(3, lambda i: (i // 2, 3 + 2 * i + 3 * (i // 2), 1 - i // 2))
    for h in range(2):
        for dp in (3, 1):
            for half in range(2):
                await_piece(h, dp, 2, half)
    images(3, lambda i: (1 - i // 2, 3 + 2 * i + 3 * (i // 2), 1 - i // 2))
    for h in range(2):
        for half in range(2):
            await_piece(h, 2, 2, half)
    images(2, lambda i: (i, 2, 1))

    span = 32 // CHUNKS * 8

    def source(k, s):
        return lax.rem(src_ref[k, s], 32)

    def sigma_of(s, unit, buf):
        for t in range(4):
            rhs = jnp.concatenate([image[k, source(k, s)] for k in (2 * t, 2 * t + 1)], axis=0)
            lhs = jnp.concatenate([scaled[2 * t, s], scaled[2 * t + 1, s]], axis=1)
            pltpu.matmul_push_rhs(rhs, t % 2, unit)
            pltpu.matmul_acc_lhs(acc[unit][buf], lhs, t % 2)

    def sigma_chunk(c):
        @pl.loop(c * (8 // CHUNKS), (c + 1) * (8 // CHUNKS))
        def _(i):
            for pair in range(2):
                at_pair = 2 * i + pair
                for e in range(2):
                    sigma_of(2 * at_pair + e, e, pair)
                    full_t[at_pair, :, e * 128 : e * 128 + 128] = full[2 * at_pair + e].T
                first, second = pltpu.matmul_pop(acc[0][pair]), pltpu.matmul_pop(acc[1][pair])
                rows = pl.ds(pl.multiple_of(at_pair * 16, 16), 16)
                for o in range(16):
                    two = jnp.concatenate([first[o * 8 : o * 8 + 8], second[o * 8 : o * 8 + 8]], axis=0).astype(BF16)
                    parts[0, o // 4, o % 4, rows, :] = two[:, :128]
                    parts[1, o % 4, o // 4, rows, :] = two[:, 128:]

    steps = ((0, 1), (1, 3))

    def rows_of(c, half):
        return pl.ds(c * span + half * (span // 2), span // 2)

    def sum1(c):
        for h in range(2):
            p, q = coords[h]
            for d, step in steps:
                start(parts.at[h, turn(q, 2), :, rows_of(c, d), :], hop1.at[h, d, c], sum_sem.at[0, h, d, c], at(h, 0, step))

    def sum2(c):
        for h in range(2):
            p, q = coords[h]
            for d, step in steps:
                arrived(hop1.at[h, d, c], sum_sem.at[0, h, d, c])
                near = turn(q, step)
                old = parts[h, near, :, rows_of(c, d), :].astype(F32)
                parts[h, near, :, rows_of(c, d), :] = (old + hop1[h, d, c].astype(F32)).astype(BF16)
                start(parts.at[h, near, :, pl.ds(c * span, span), :], hop2.at[h, d, c], sum_sem.at[1, h, d, c], at(h, 0, step))

    def sum3(c):
        for h in range(2):
            p, q = coords[h]
            for d, step in steps:
                arrived(hop2.at[h, d, c], sum_sem.at[1, h, d, c])
            rows = pl.ds(c * span, span)
            total = parts[h, q, :, rows, :].astype(F32) + hop2[h, 0, c].astype(F32) + hop2[h, 1, c].astype(F32)
            kept[h, :, rows, :] = total.astype(BF16)
            for d, step in steps:
                start(kept.at[h, turn(p, 2), rows_of(c, d), :], hop3.at[h, d, c], sum_sem.at[2, h, d, c], at(h, step, 0))

    def sum4(c):
        for h in range(2):
            p, q = coords[h]
            for d, step in steps:
                arrived(hop3.at[h, d, c], sum_sem.at[2, h, d, c])
                near = turn(p, step)
                old = kept[h, near, rows_of(c, d), :].astype(F32)
                kept[h, near, rows_of(c, d), :] = (old + hop3[h, d, c].astype(F32)).astype(BF16)
                start(kept.at[h, near, pl.ds(c * span, span), :], hop4.at[h, d, c], sum_sem.at[3, h, d, c], at(h, step, 0))

    def sum5(c):
        for h in range(2):
            p, q = coords[h]
            for d, step in steps:
                arrived(hop4.at[h, d, c], sum_sem.at[3, h, d, c])
            rows = pl.ds(c * span, span)
            total = kept[h, p, rows, :].astype(F32) + hop4[h, 0, c].astype(F32) + hop4[h, 1, c].astype(F32)
            sig_ref[rows, pl.ds(h * 128, 128)] = total * (128 ** -0.5)

    def half_product(ks):
        @pl.loop(0, 4)
        def _(i):
            for e in range(4):
                for j in range(2):
                    none = jnp.zeros((128, 128), BF16)
                    one, two = left[ks[j], 8 * i + 2 * e], left[ks[j], 8 * i + 2 * e + 1]
                    rhs = jnp.concatenate(
                        [jnp.concatenate([one, none], axis=1), jnp.concatenate([none, two], axis=1)], axis=0
                    )
                    pltpu.matmul_push_rhs(rhs, e % 2, j)
                    for half in range(2):
                        buf = acc[j][e % 2 * 2 + half]
                        pltpu.matmul_acc_lhs(
                            buf, full_t[4 * i + e, half * 128 : half * 128 + 128, :], e % 2 if half == 0 else None
                        )
                for j in range(2):
                    for half in range(2):
                        zed[j, 4 * i + e, half * 128 : half * 128 + 128, :] = pltpu.matmul_pop(
                            acc[j][e % 2 * 2 + half]
                        ).astype(BF16)

    def renorm(ks, slot):
        @pl.loop(0, 4)
        def _(i):
            for e in range(4):
                for j in range(2):
                    rhs = jnp.concatenate([full[source(ks[j], 8 * i + 2 * e + n)] for n in range(2)], axis=0)
                    pltpu.matmul_push_rhs(rhs, e % 2, j)
                    for half in range(2):
                        pltpu.matmul_acc_lhs(
                            acc[j][half], zed[j, 4 * i + e, half * 128 : half * 128 + 128, :], e % 2 if half == 0 else None
                        )

        for j in range(2):
            for half in range(2):
                block[slot + j, half * 128 : half * 128 + 128, :] = (
                    pltpu.matmul_pop(acc[j][half]) * (4096 ** -0.5)
                ).astype(BF16)

    def push(src, dst, recv_sem, target):
        copy = pltpu.make_async_remote_copy(
            src_ref=src, dst_ref=dst, send_sem=send_sem.at[len(sent)], recv_sem=recv_sem,
            device_id=(op, target), device_id_type=MESH,
        )
        copy.start()
        sent.append(copy)

    def ship(slot, dy, target):
        push(block.at[slot], ren_ref.at[sec], swap_sem.at[dy, core], target)

    def half_rows(d):
        return pl.ds(d * 128, 128)

    def ship_far():
        for j in range(2):
            for d, step in steps:
                push(block.at[j, half_rows(d)], relay.at[d, j], relay_sem.at[d, j], turn(y, step) * 2 + core)

    def relay_far():
        for j in range(2):
            for d, step in steps:
                arrived(relay.at[d, j], relay_sem.at[d, j])
                sender = turn(y, 4 - step) * 2 + core
                push(relay.at[d, j], ren_ref.at[sender, half_rows(d)], far_sem.at[d, core], turn(y, step) * 2 + j)

    def swapped(dy, sender_core):
        sender = turn(y, 4 - dy) * 2 + sender_core
        arrived(ren_ref.at[sender], swap_sem.at[dy, sender_core])

    far = [turn(y, 2) * 2 + j for j in range(2)]
    near = [[turn(y, dy) * 2 + j for dy in (1, 3)] for j in range(2)]
    here = [2 * y + j for j in range(2)]

    sigma_chunk(0)
    sum1(0)
    sigma_chunk(1)
    sum1(1)
    sigma_chunk(2)
    sum1(2)
    sum2(0)
    sigma_chunk(3)
    sum1(3)
    sum2(1)
    half_product(far)
    sum2(2)
    renorm(far, 0)
    ship_far()
    sum2(3)
    sum3(0)
    half_product(near[0])
    sum3(1)
    renorm(near[0], 2)
    ship(2, 1, near[0][0])
    ship(3, 3, near[0][1])
    sum3(2)
    relay_far()
    half_product(near[1])
    sum3(3)
    sum4(0)
    renorm(near[1], 4)
    ship(4, 1, near[1][0])
    ship(5, 3, near[1][1])
    sum4(1)
    sum4(2)
    sum5(0)
    half_product(here)
    sum4(3)
    sum5(1)
    renorm(here, 6)
    ship(7 - core, 0, 2 * y + 1 - core)
    own = pltpu.make_async_copy(block.at[6 + core], ren_ref.at[sec], own_sem)
    own.start()
    sum5(2)
    sum5(3)
    for dy in (1, 3):
        for c in range(2):
            swapped(dy, c)
    for c in range(2):
        for d in range(2):
            arrived(ren_ref.at[turn(y, 2) * 2 + c, half_rows(d)], far_sem.at[d, c])
    swapped(0, 1 - core)
    own.wait()
    for copy in sent:
        copy.wait_send()


def with_totals(*refs):
    totals = [pltpu.ACC(unit)((128, 256), F32) for unit in (0, 0, 0, 0, 1, 1, 1, 1)]
    pl.run_scoped(functools.partial(kernel, *refs), *totals)


def finish(sig_ref, ren_ref, sigma_ref, renorm_ref, sig, sigma, narrow, wide, in_sem, out_sem):
    come = [pltpu.make_async_copy(ren_ref.at[i], narrow.at[i], in_sem.at[i]) for i in range(8)]
    come.append(pltpu.make_async_copy(sig_ref, sig, in_sem.at[8]))
    go = [pltpu.make_async_copy(wide.at[i], renorm_ref.at[i], out_sem.at[i]) for i in range(8)]
    go.append(pltpu.make_async_copy(sigma, sigma_ref, out_sem.at[8]))
    for copy in come:
        copy.start()
    for i in range(8):
        come[i].wait()
        wide[i] = narrow[i].astype(F32)
        go[i].start()
    come[8].wait()
    sigma[...] = sig[...].astype(BF16)
    go[8].start()
    for copy in go:
        copy.wait()


def body(psi, left_env, right_env, source, coupling):
    vm = pltpu.VMEM
    rows = 256 // CHUNKS
    sig, ren = pl.pallas_call(
        with_totals,
        out_shape=(jax.ShapeDtypeStruct((256, 256), F32), jax.ShapeDtypeStruct((8, 256, 256), BF16)),
        in_specs=[pl.BlockSpec(memory_space=pl.ANY)] * 3 + [pl.BlockSpec(memory_space=pltpu.SMEM)] * 2,
        out_specs=(pl.BlockSpec(memory_space=pltpu.VMEM), pl.BlockSpec(memory_space=pl.ANY)),
        scratch_shapes=[
            vm((8, 32, 128, 128), BF16),
            vm((8, 32, 128, 128), BF16),
            vm((8, 256, 256), BF16),
            vm((2, 16, 128, 256), BF16),
            vm((32, 128, 256), BF16),
            vm((16, 256, 256), BF16),
            vm((8, 32, 128, 256), BF16),
            vm((2, 16, 256, 256), BF16),
            vm((2, 4, 4, 256, 128), BF16),
            vm((8, 256, 256), BF16),
            vm((2, 2, CHUNKS, 4, rows // 2, 128), BF16),
            vm((2, 2, CHUNKS, 4, rows, 128), BF16),
            vm((2, 4, 256, 128), BF16),
            vm((2, 2, CHUNKS, rows // 2, 128), BF16),
            vm((2, 2, CHUNKS, rows, 128), BF16),
            vm((2, 2, 128, 256), BF16),
            pltpu.SemaphoreType.DMA((4,)),
            pltpu.SemaphoreType.DMA((128,)),
            pltpu.SemaphoreType.DMA((2, 16, 2)),
            pltpu.SemaphoreType.DMA((4, 2, 2, CHUNKS)),
            pltpu.SemaphoreType.DMA((4, 2)),
            pltpu.SemaphoreType.DMA((2, 2)),
            pltpu.SemaphoreType.DMA((2, 2)),
            pltpu.SemaphoreType.DMA,
        ],
        compiler_params=pltpu.CompilerParams(
            collective_id=0, has_side_effects=True, vmem_limit_bytes=60 * 1024 * 1024
        ),
        cost_estimate=pl.CostEstimate(flops=13 * 10**9, bytes_accessed=12 * 2**20, transcendentals=0),
        name="dmrg_step",
    )(psi.reshape(256, 256), left_env, right_env.reshape(8, 256, 256), source, coupling)
    sigma, renorm = pl.pallas_call(
        finish,
        out_shape=(jax.ShapeDtypeStruct((256, 256), BF16), jax.ShapeDtypeStruct((8, 256, 256), F32)),
        in_specs=[pl.BlockSpec(memory_space=pl.ANY)] * 2,
        out_specs=(pl.BlockSpec(memory_space=pl.ANY), pl.BlockSpec(memory_space=pl.ANY)),
        scratch_shapes=[
            vm((256, 256), F32),
            vm((256, 256), BF16),
            vm((8, 256, 256), BF16),
            vm((8, 256, 256), F32),
            pltpu.SemaphoreType.DMA((9,)),
            pltpu.SemaphoreType.DMA((9,)),
        ],
        compiler_params=pltpu.CompilerParams(vmem_limit_bytes=60 * 1024 * 1024),
        name="finish",
    )(sig, ren)
    return sigma.reshape(32, 8, 256), renorm[None]


def solution(mesh):
    placed = (
        P("sec", "op", None),
        P("op", "sec", None, None),
        P("op", "sec", None, None),
        P("op", "sec"),
        P("op", "sec"),
    )
    return jax.shard_map(
        body,
        mesh=mesh,
        in_specs=placed,
        out_specs=(P("sec", "op", None), P(("op", "sec"), None, None, None)),
        check_vma=False,
    )
```

time: 255 us -> 58.2 us (0.23)
  blocking collectives: 103 us -> 0 us
  matrix products: 61.8 us -> 0 us
  Pallas kernels: 0 us -> 57.1 us
  waiting for transfers between devices: 51.6 us -> 0 us
  local copies, waits for them, and re-layouts: 14.9 us -> 0 us
  between operations: 14.1 us -> 0.64 us
  starting transfers between devices: 4.34 us -> 0 us
  other arithmetic: 4.02 us -> 0 us
    psum x1 -> x0, blocking collectives: 103 us -> none  [body(): summed = lax.psum(partial_sigma, 'op')]
    dot_general x4 -> x0, matrix products: 61.8 us -> none  [the longest x1 21.1 us: body(): jnp.einsum('ksab,ksbm->ksam', left_env, picked, preferred_element_type=jn...]
    pallas_call x0 -> x2, Pallas kernels: none -> 57.1 us  [the longest x1 54.7 us: body(): pl.pallas_call(with_totals, out_shape=(jax.ShapeDtypeStruct((256, 256), F...]
    all_gather x1 -> x0, waiting for transfers between devices: 50.9 us -> none  [body(): full = lax.all_gather(psi, 'op', axis=1, tiled=True)]
    gather x1 -> x0, local copies, waits for them, and re-layouts: 11.3 us -> none  [body(): picked = full[local_src]]
    all_to_all x1 -> x0, starting transfers between devices: 4.3 us -> none  [body(): lax.all_to_all(group_renorm[:, None], 'sec', split_axis=0, concat_axis=1,...]
    mul x1 -> x0, other arithmetic: 2.62 us -> none  [body(): partial_sigma = jnp.einsum('ks,ksan->san', coef, image) * kops ** (-0.5)]
  transfers between devices with their start and end apart: 2 -> 0, of which waited for: 1 -> 0; matrix products, arithmetic and copies ran while one was open for 1% -> 0% of each run, Pallas kernels for 0% -> 0%
where the time goes in v1:
time: 58.2 us; the launch traced here: 57.7 us
  Pallas kernels  57.1 us (98%)
  between operations  0.64 us (1%)
    pallas_call x1, Pallas kernels, body(): pl.pallas_call(with_totals, out_shape=(jax.ShapeDtypeStruct((256, 256), F...  54.7 us
    pallas_call x1, Pallas kernels, body(): pl.pallas_call(finish, out_shape=(jax.ShapeDtypeStruct((256, 256), BF16),...  2.42 us

profile of v1, /device:TPU:0, one launch (start us, length us, event | category | flops | bytes accessed | tf_op | source)
XLA Modules:
  0.0 57.7 jit_solution(11640418223567334238)
XLA Ops:
  0.6 54.7 %dmrg_step.1 = (f32[256,256]{1,0:T(8,128)}, bf16[8,256,256]{2,1,0:T(8,128)(2,1)}) custom-call(bf16[256,256]{1,0:T(8,128)(2,1)} %bitcast.6, bf16[8,32,128,128]{3,2,1,0:T(8,128)(2,1)} %refs_1_.1, bf16[8,256,256]{2,1,0:T(8,128)(2,1)} %bitcast.5, s32[8,32]{1,0:T(8,128)} %refs_3_.1, s32[8,32]{1,0:T(8,128)} %refs_4_.1), custom_call_target="tpu_custom_call" | custom-call | flops 12999999488 | bytes 12582912 | tf_op jit(solution)/shard_map/dmrg_step/pallas_call | solution.py:408
  55.3 2.4 %finish.1 = (bf16[256,256]{1,0:T(8,128)(2,1)}, f32[8,256,256]{2,1,0:T(8,128)}) custom-call(f32[256,256]{1,0:T(8,128)} %get-tuple-element.6.sig_ref, bf16[8,256,256]{2,1,0:T(8,128)(2,1)} %get-tuple-element.7.ren_ref), custom_call_target="tpu_custom_call" | custom-call | tf_op jit(solution)/shard_map/finish/pallas_call | solution.py:445

commit v2 on v1

--- a/solution.py
+++ b/solution.py
@@ -35,8 +35,8 @@
     loads = [
         pltpu.make_async_copy(psi_ref.at[pl.ds(h * 128, 128)], got.at[h, op], load_sem.at[h]) for h in range(2)
     ]
-    loads.append(pltpu.make_async_copy(left_ref, left, load_sem.at[2]))
-    loads.append(pltpu.make_async_copy(right_ref, right, load_sem.at[3]))
+    loads.append(pltpu.make_async_copy(right_ref, right, load_sem.at[2]))
+    loads += [pltpu.make_async_copy(left_ref.at[k], left.at[k], load_sem.at[3 + k]) for k in range(8)]
     for copy in loads:
         copy.start()
 
@@ -91,6 +91,9 @@
             pass_on(h, 0, 0, None, 0, sq)
 
     def scale(part):
+        for k in (2 * part, 2 * part + 1):
+            loads[3 + k].wait()
+
         @pl.loop(2 * part, 2 * part + 2)
         def _(k):
             @pl.loop(0, 32, unroll=8)
@@ -127,8 +130,6 @@
             j = x // 2
             pair_image(h, lax.rem(z + dz, 4), j + other * (1 - 2 * j))
 
-    loads[2].wait()
-    scale(0)
     for h in range(2):
         for dp, half, sp in ((3, 0, 1), (1, 1, -1)):
             await_piece(h, dp, 0, None)
@@ -139,8 +140,9 @@
         for dq, half, sq in ((3, 0, 1), (1, 1, -1)):
             await_piece(h, 0, dq, None)
             pass_on(h, 0, dq, half, 0, sq)
-    loads[3].wait()
+    loads[2].wait()
     images(2, lambda i: (i, 0, 0))
+    scale(0)
     for h in range(2):
         await_piece(h, 2, 0, 0)
         await_piece(h, 2, 0, 1)
@@ -193,7 +195,6 @@
                 at_pair = 2 * i + pair
                 for e in range(2):
                     sigma_of(2 * at_pair + e, e, pair)
-                    full_t[at_pair, :, e * 128 : e * 128 + 128] = full[2 * at_pair + e].T
                 first, second = pltpu.matmul_pop(acc[0][pair]), pltpu.matmul_pop(acc[1][pair])
                 rows = pl.ds(pl.multiple_of(at_pair * 16, 16), 16)
                 for o in range(16):
@@ -252,38 +253,35 @@
             total = kept[h, p, rows, :].astype(F32) + hop4[h, 0, c].astype(F32) + hop4[h, 1, c].astype(F32)
             sig_ref[rows, pl.ds(h * 128, 128)] = total * (128 ** -0.5)
 
-    def half_product(ks):
+    def mix(ks, turning=False):
+        @pl.loop(0, 4)
+        def _(i):
+            none = jnp.zeros((128, 128), BF16)
+            for e in range(4):
+                at_pair = 4 * i + e
+                if turning:
+                    for n in range(2):
+                        full_t[at_pair, :, n * 128 : n * 128 + 128] = full[2 * at_pair + n].T
+                for j in range(2):
+                    rhs = jnp.concatenate([full[source(ks[j], 2 * at_pair + n)] for n in range(2)], axis=0)
+                    pltpu.matmul_push_rhs(rhs, e % 2, j)
+                    for n in range(2):
+                        one = left[ks[j], 2 * at_pair + n]
+                        lhs = jnp.concatenate([one, none] if n == 0 else [none, one], axis=1)
+                        pltpu.matmul_acc_lhs(acc[j][e % 2 * 2 + n], lhs, e % 2 if n == 0 else None)
+                for j in range(2):
+                    for n in range(2):
+                        zed[j, at_pair, n * 128 : n * 128 + 128, :] = pltpu.matmul_pop(acc[j][e % 2 * 2 + n]).astype(BF16)
+
+    def renorm(slot):
         @pl.loop(0, 4)
         def _(i):
             for e in range(4):
                 for j in range(2):
-                    none = jnp.zeros((128, 128), BF16)
-                    one, two = left[ks[j], 8 * i + 2 * e], left[ks[j], 8 * i + 2 * e + 1]
-                    rhs = jnp.concatenate(
-                        [jnp.concatenate([one, none], axis=1), jnp.concatenate([none, two], axis=1)], axis=0
-                    )
-                    pltpu.matmul_push_rhs(rhs, e % 2, j)
-                    for half in range(2):
-                        buf = acc[j][e % 2 * 2 + half]
-                        pltpu.matmul_acc_lhs(
-                            buf, full_t[4 * i + e, half * 128 : half * 128 + 128, :], e % 2 if half == 0 else None
-                        )
-                for j in range(2):
-                    for half in range(2):
-                        zed[j, 4 * i + e, half * 128 : half * 128 + 128, :] = pltpu.matmul_pop(
-                            acc[j][e % 2 * 2 + half]
-                        ).astype(BF16)
-
-    def renorm(ks, slot):
-        @pl.loop(0, 4)
-        def _(i):
-            for e in range(4):
-                for j in range(2):
-                    rhs = jnp.concatenate([full[source(ks[j], 8 * i + 2 * e + n)] for n in range(2)], axis=0)
-                    pltpu.matmul_push_rhs(rhs, e % 2, j)
+                    pltpu.matmul_push_rhs(zed[j, 4 * i + e], e % 2, j)
                     for half in range(2):
                         pltpu.matmul_acc_lhs(
-                            acc[j][half], zed[j, 4 * i + e, half * 128 : half * 128 + 128, :], e % 2 if half == 0 else None
+                            acc[j][half], full_t[4 * i + e, half * 128 : half * 128 + 128, :], e % 2 if half == 0 else None
                         )
 
         for j in range(2):
@@ -330,41 +328,41 @@
     sum1(0)
     sigma_chunk(1)
     sum1(1)
+    mix(far, turning=True)
+    sum2(0)
+    renorm(0)
+    ship_far()
+    sum2(1)
     sigma_chunk(2)
     sum1(2)
-    sum2(0)
     sigma_chunk(3)
     sum1(3)
-    sum2(1)
-    half_product(far)
+    sum3(0)
+    mix(near[0])
     sum2(2)
-    renorm(far, 0)
-    ship_far()
-    sum2(3)
-    sum3(0)
-    half_product(near[0])
     sum3(1)
-    renorm(near[0], 2)
+    renorm(2)
     ship(2, 1, near[0][0])
     ship(3, 3, near[0][1])
+    sum2(3)
+    sum4(0)
+    relay_far()
+    mix(near[1])
     sum3(2)
-    relay_far()
-    half_product(near[1])
-    sum3(3)
-    sum4(0)
-    renorm(near[1], 4)
+    sum4(1)
+    renorm(4)
     ship(4, 1, near[1][0])
     ship(5, 3, near[1][1])
-    sum4(1)
+    sum3(3)
+    sum5(0)
+    mix(here)
     sum4(2)
-    sum5(0)
-    half_product(here)
-    sum4(3)
     sum5(1)
-    renorm(here, 6)
+    renorm(6)
     ship(7 - core, 0, 2 * y + 1 - core)
     own = pltpu.make_async_copy(block.at[6 + core], ren_ref.at[sec], own_sem)
     own.start()
+    sum4(3)
     sum5(2)
     sum5(3)
     for dy in (1, 3):
@@ -427,7 +425,7 @@
             vm((2, 2, CHUNKS, rows // 2, 128), BF16),
             vm((2, 2, CHUNKS, rows, 128), BF16),
             vm((2, 2, 128, 256), BF16),
-            pltpu.SemaphoreType.DMA((4,)),
+            pltpu.SemaphoreType.DMA((11,)),
             pltpu.SemaphoreType.DMA((128,)),
             pltpu.SemaphoreType.DMA((2, 16, 2)),
             pltpu.SemaphoreType.DMA((4, 2, 2, CHUNKS)),

time: 58.2 us -> 56.6 us (0.973)
  Pallas kernels: 57.1 us -> 55.8 us
    pallas_call x1, Pallas kernels: 54.7 us -> 53.3 us  [body(): pl.pallas_call(with_totals, out_shape=(jax.ShapeDtypeStruct((256, 256), F...]
where the time goes in v2:
time: 56.6 us; the launch traced here: 56.4 us
  Pallas kernels  55.8 us (99%)
  between operations  0.64 us (1%)
    pallas_call x1, Pallas kernels, body(): pl.pallas_call(with_totals, out_shape=(jax.ShapeDtypeStruct((256, 256), F...  53.3 us
    pallas_call x1, Pallas kernels, body(): pl.pallas_call(finish, out_shape=(jax.ShapeDtypeStruct((256, 256), BF16),...  2.42 us

profile of v2, /device:TPU:0, one launch (start us, length us, event | category | flops | bytes accessed | tf_op | source)
XLA Modules:
  0.0 56.4 jit_solution(2160231316437838354)
XLA Ops:
  0.6 53.3 %dmrg_step.1 = (f32[256,256]{1,0:T(8,128)}, bf16[8,256,256]{2,1,0:T(8,128)(2,1)}) custom-call(bf16[256,256]{1,0:T(8,128)(2,1)} %bitcast.6, bf16[8,32,128,128]{3,2,1,0:T(8,128)(2,1)} %refs_1_.1, bf16[8,256,256]{2,1,0:T(8,128)(2,1)} %bitcast.5, s32[8,32]{1,0:T(8,128)} %refs_3_.1, s32[8,32]{1,0:T(8,128)} %refs_4_.1), custom_call_target="tpu_custom_call" | custom-call | flops 12999999488 | bytes 12582912 | tf_op jit(solution)/shard_map/dmrg_step/pallas_call | solution.py:406
  54.0 2.4 %finish.1 = (bf16[256,256]{1,0:T(8,128)(2,1)}, f32[8,256,256]{2,1,0:T(8,128)}) custom-call(f32[256,256]{1,0:T(8,128)} %get-tuple-element.6.sig_ref, bf16[8,256,256]{2,1,0:T(8,128)(2,1)} %get-tuple-element.7.ren_ref), custom_call_target="tpu_custom_call" | custom-call | tf_op jit(solution)/shard_map/finish/pallas_call | solution.py:443

commit v3 on v2

--- a/solution.py
+++ b/solution.py
@@ -11,7 +11,7 @@
 MESH = pl.DeviceIdType.MESH
 F32 = jnp.float32
 BF16 = jnp.bfloat16
-CHUNKS = 4
+CHUNKS = 2
 
 
 def turn(a, step):
@@ -47,8 +47,6 @@
         pl.semaphore_signal(barrier, inc=1, device_id=peer, device_id_type=MESH)
     pl.semaphore_wait(barrier, len(peers))
 
-    sent = []
-
     def place(h, p, q):
         return q * 4 + p if h == 0 else p * 4 + q
 
@@ -56,13 +54,11 @@
         p, q = coords[h]
         return place(h, turn(p, dp), turn(q, dq))
 
-    def start(src, dst, recv_sem, target):
-        copy = pltpu.make_async_remote_copy(
-            src_ref=src, dst_ref=dst, send_sem=send_sem.at[len(sent)], recv_sem=recv_sem,
+    def start(src, dst, kind, recv_sem, target):
+        pltpu.make_async_remote_copy(
+            src_ref=src, dst_ref=dst, send_sem=send_sem.at[kind], recv_sem=recv_sem,
             device_id=(target, sec), device_id_type=MESH,
-        )
-        copy.start()
-        sent.append(copy)
+        ).start()
 
     def arrived(dst, recv_sem):
         pltpu.make_async_remote_copy(
@@ -77,7 +73,7 @@
     def pass_on(h, dp, dq, half, sp, sq):
         ref = piece(h, dp, dq, half)
         rel = (dp - sp) % 4 * 4 + (dq - sq) % 4
-        start(ref, ref, gather_sem.at[h, rel, 0 if half is None else half], at(h, sp % 4, sq % 4))
+        start(ref, ref, h, gather_sem.at[h, rel, 0 if half is None else half], at(h, sp % 4, sq % 4))
 
     def await_piece(h, dp, dq, half):
         arrived(piece(h, dp, dq, half), gather_sem.at[h, dp * 4 + dq, 0 if half is None else half])
@@ -211,7 +207,7 @@
         for h in range(2):
             p, q = coords[h]
             for d, step in steps:
-                start(parts.at[h, turn(q, 2), :, rows_of(c, d), :], hop1.at[h, d, c], sum_sem.at[0, h, d, c], at(h, 0, step))
+                start(parts.at[h, turn(q, 2), :, rows_of(c, d), :], hop1.at[h, d, c], 2, sum_sem.at[0, h, d, c], at(h, 0, step))
 
     def sum2(c):
         for h in range(2):
@@ -221,7 +217,7 @@
                 near = turn(q, step)
                 old = parts[h, near, :, rows_of(c, d), :].astype(F32)
                 parts[h, near, :, rows_of(c, d), :] = (old + hop1[h, d, c].astype(F32)).astype(BF16)
-                start(parts.at[h, near, :, pl.ds(c * span, span), :], hop2.at[h, d, c], sum_sem.at[1, h, d, c], at(h, 0, step))
+                start(parts.at[h, near, :, pl.ds(c * span, span), :], hop2.at[h, d, c], 3, sum_sem.at[1, h, d, c], at(h, 0, step))
 
     def sum3(c):
         for h in range(2):
@@ -232,7 +228,7 @@
             total = parts[h, q, :, rows, :].astype(F32) + hop2[h, 0, c].astype(F32) + hop2[h, 1, c].astype(F32)
             kept[h, :, rows, :] = total.astype(BF16)
             for d, step in steps:
-                start(kept.at[h, turn(p, 2), rows_of(c, d), :], hop3.at[h, d, c], sum_sem.at[2, h, d, c], at(h, step, 0))
+                start(kept.at[h, turn(p, 2), rows_of(c, d), :], hop3.at[h, d, c], 4, sum_sem.at[2, h, d, c], at(h, step, 0))
 
     def sum4(c):
         for h in range(2):
@@ -242,7 +238,7 @@
                 near = turn(p, step)
                 old = kept[h, near, rows_of(c, d), :].astype(F32)
                 kept[h, near, rows_of(c, d), :] = (old + hop3[h, d, c].astype(F32)).astype(BF16)
-                start(kept.at[h, near, pl.ds(c * span, span), :], hop4.at[h, d, c], sum_sem.at[3, h, d, c], at(h, step, 0))
+                start(kept.at[h, near, pl.ds(c * span, span), :], hop4.at[h, d, c], 5, sum_sem.at[3, h, d, c], at(h, step, 0))
 
     def sum5(c):
         for h in range(2):
@@ -290,16 +286,14 @@
                     pltpu.matmul_pop(acc[j][half]) * (4096 ** -0.5)
                 ).astype(BF16)
 
-    def push(src, dst, recv_sem, target):
-        copy = pltpu.make_async_remote_copy(
-            src_ref=src, dst_ref=dst, send_sem=send_sem.at[len(sent)], recv_sem=recv_sem,
+    def push(src, dst, kind, recv_sem, target):
+        pltpu.make_async_remote_copy(
+            src_ref=src, dst_ref=dst, send_sem=send_sem.at[kind], recv_sem=recv_sem,
             device_id=(op, target), device_id_type=MESH,
-        )
-        copy.start()
-        sent.append(copy)
+        ).start()
 
     def ship(slot, dy, target):
-        push(block.at[slot], ren_ref.at[sec], swap_sem.at[dy, core], target)
+        push(block.at[slot], ren_ref.at[sec], 6, swap_sem.at[dy, core], target)
 
     def half_rows(d):
         return pl.ds(d * 128, 128)
@@ -307,14 +301,14 @@
     def ship_far():
         for j in range(2):
             for d, step in steps:
-                push(block.at[j, half_rows(d)], relay.at[d, j], relay_sem.at[d, j], turn(y, step) * 2 + core)
+                push(block.at[j, half_rows(d)], relay.at[d, j], 6, relay_sem.at[d, j], turn(y, step) * 2 + core)
 
     def relay_far():
         for j in range(2):
             for d, step in steps:
                 arrived(relay.at[d, j], relay_sem.at[d, j])
                 sender = turn(y, 4 - step) * 2 + core
-                push(relay.at[d, j], ren_ref.at[sender, half_rows(d)], far_sem.at[d, core], turn(y, step) * 2 + j)
+                push(relay.at[d, j], ren_ref.at[sender, half_rows(d)], 7, far_sem.at[d, core], turn(y, step) * 2 + j)
 
     def swapped(dy, sender_core):
         sender = turn(y, 4 - dy) * 2 + sender_core
@@ -333,38 +327,26 @@
     renorm(0)
     ship_far()
     sum2(1)
-    sigma_chunk(2)
-    sum1(2)
-    sigma_chunk(3)
-    sum1(3)
+    mix(near[0])
     sum3(0)
-    mix(near[0])
-    sum2(2)
-    sum3(1)
     renorm(2)
     ship(2, 1, near[0][0])
     ship(3, 3, near[0][1])
-    sum2(3)
+    relay_far()
     sum4(0)
-    relay_far()
     mix(near[1])
-    sum3(2)
-    sum4(1)
+    sum3(1)
     renorm(4)
     ship(4, 1, near[1][0])
     ship(5, 3, near[1][1])
-    sum3(3)
     sum5(0)
     mix(here)
-    sum4(2)
-    sum5(1)
+    sum4(1)
     renorm(6)
     ship(7 - core, 0, 2 * y + 1 - core)
     own = pltpu.make_async_copy(block.at[6 + core], ren_ref.at[sec], own_sem)
     own.start()
-    sum4(3)
-    sum5(2)
-    sum5(3)
+    sum5(1)
     for dy in (1, 3):
         for c in range(2):
             swapped(dy, c)
@@ -373,8 +355,9 @@
             arrived(ren_ref.at[turn(y, 2) * 2 + c, half_rows(d)], far_sem.at[d, c])
     swapped(0, 1 - core)
     own.wait()
-    for copy in sent:
-        copy.wait_send()
+    all_sent = (got.at[0, pl.ds(0, 15)], got.at[1, pl.ds(0, 15)], hop1, hop2, hop3, hop4, block.at[pl.ds(0, 7)], relay)
+    for kind, ref in enumerate(all_sent):
+        pltpu.make_async_copy(ref, ref, send_sem.at[kind]).wait()
 
 
 def with_totals(*refs):
@@ -426,7 +409,7 @@
             vm((2, 2, CHUNKS, rows, 128), BF16),
             vm((2, 2, 128, 256), BF16),
             pltpu.SemaphoreType.DMA((11,)),
-            pltpu.SemaphoreType.DMA((128,)),
+            pltpu.SemaphoreType.DMA((8,)),
             pltpu.SemaphoreType.DMA((2, 16, 2)),
             pltpu.SemaphoreType.DMA((4, 2, 2, CHUNKS)),
             pltpu.SemaphoreType.DMA((4, 2)),

time: 56.6 us -> 55.3 us (0.977)
  Pallas kernels: 55.8 us -> 54.4 us
    pallas_call x1, Pallas kernels: 53.3 us -> 51.9 us  [body(): pl.pallas_call(with_totals, out_shape=(jax.ShapeDtypeStruct((256, 256), F...]
where the time goes in v3:
time: 55.3 us; the launch traced here: 55 us
  Pallas kernels  54.4 us (98%)
  between operations  0.64 us (1%)
    pallas_call x1, Pallas kernels, body(): pl.pallas_call(with_totals, out_shape=(jax.ShapeDtypeStruct((256, 256), F...  51.9 us
    pallas_call x1, Pallas kernels, body(): pl.pallas_call(finish, out_shape=(jax.ShapeDtypeStruct((256, 256), BF16),...  2.42 us

profile of v3, /device:TPU:0, one launch (start us, length us, event | category | flops | bytes accessed | tf_op | source)
XLA Modules:
  0.0 55.0 jit_solution(12310299648520827988)
XLA Ops:
  0.6 51.9 %dmrg_step.1 = (f32[256,256]{1,0:T(8,128)}, bf16[8,256,256]{2,1,0:T(8,128)(2,1)}) custom-call(bf16[256,256]{1,0:T(8,128)(2,1)} %bitcast.6, bf16[8,32,128,128]{3,2,1,0:T(8,128)(2,1)} %refs_1_.1, bf16[8,256,256]{2,1,0:T(8,128)(2,1)} %bitcast.5, s32[8,32]{1,0:T(8,128)} %refs_3_.1, s32[8,32]{1,0:T(8,128)} %refs_4_.1), custom_call_target="tpu_custom_call" | custom-call | flops 12999999488 | bytes 12582912 | tf_op jit(solution)/shard_map/dmrg_step/pallas_call | solution.py:389
  52.6 2.4 %finish.1 = (bf16[256,256]{1,0:T(8,128)(2,1)}, f32[8,256,256]{2,1,0:T(8,128)}) custom-call(f32[256,256]{1,0:T(8,128)} %get-tuple-element.6.sig_ref, bf16[8,256,256]{2,1,0:T(8,128)(2,1)} %get-tuple-element.7.ren_ref), custom_call_target="tpu_custom_call" | custom-call | tf_op jit(solution)/shard_map/finish/pallas_call | solution.py:426

commit v4 on v3

--- a/solution.py
+++ b/solution.py
@@ -24,9 +24,9 @@
     left, scaled, right, got, full, full_t, image, zed, parts, block,
     hop1, hop2, kept, hop3, hop4, relay,
     load_sem, send_sem, gather_sem, sum_sem, swap_sem, relay_sem, far_sem, own_sem,
-    acc00, acc01, acc02, acc03, acc10, acc11, acc12, acc13,
+    *totals,
 ):
-    acc = ((acc00, acc01, acc02, acc03), (acc10, acc11, acc12, acc13))
+    acc = (totals[:8], totals[8:])
     op, sec = lax.axis_index("op"), lax.axis_index("sec")
     z, x = op // 4, op % 4
     y, core = sec // 2, sec % 2
@@ -100,31 +100,56 @@
                 )
                 scaled[k, s] = (left[k, s].astype(F32) * coef).astype(BF16)
 
-    def pair_image(h, zz, j):
-        to = pl.ds(pl.multiple_of(zz * 32 + j * 16, 16), 16)
-
-        def put(ref, first, second):
-            for s in range(16):
-                two = jnp.concatenate([first[s * 8 : s * 8 + 8], second[s * 8 : s * 8 + 8]], axis=0)
-                ref[h * 16 + s, to, :] = two.astype(BF16)
-
-        def rows_in(o):
-            return got[h, zz * 4 + 2 * j + o]
-
-        put(full, rows_in(0).astype(F32), rows_in(1).astype(F32))
-        for k in range(8):
-            unit, reg = k % 2, k // 2 % 2
-            pltpu.matmul_push_rhs(right[k], reg, unit)
-            for o in range(2):
-                pltpu.matmul_acc_lhs(acc[unit][2 * reg + o], rows_in(o), reg if o == 0 else None)
-            put(image.at[k], pltpu.matmul_pop(acc[unit][2 * reg]), pltpu.matmul_pop(acc[unit][2 * reg + 1]))
+    def feed(unit, base, lhs, reg):
+        for n in range(lhs.shape[0] // 64):
+            pltpu.matmul_acc_lhs(acc[unit][base + n], lhs[n * 64 : n * 64 + 64], reg if n == 0 else None)
+
+    def in_turns(steps, issue, drain, unroll):
+        issue(0, 0)
+
+        @pl.loop(0, steps // unroll - 1)
+        def _(i):
+            for u in range(unroll):
+                issue(i * unroll + u + 1, (u + 1) % unroll)
+                drain(i * unroll + u, u)
+
+        for u in range(unroll):
+            t = steps - unroll + u
+            if u + 1 < unroll:
+                issue(t + 1, u + 1)
+            drain(t, u)
 
     def images(count, which):
-        @pl.loop(0, count)
-        def _(i):
+        def place_of(i):
             h, dz, other = which(i)
             j = x // 2
-            pair_image(h, lax.rem(z + dz, 4), j + other * (1 - 2 * j))
+            j = j + other * (1 - 2 * j)
+            zz = lax.rem(z + dz, 4)
+            return h, zz * 4 + 2 * j, pl.ds(pl.multiple_of(zz * 32 + j * 16, 16), 16)
+
+        def put(ref, h, to, first, second, at_sector):
+            for s in range(8):
+                two = jnp.concatenate([first[s * 8 : s * 8 + 8], second[s * 8 : s * 8 + 8]], axis=0)
+                ref[h * 16 + at_sector + s, to, :] = two.astype(BF16)
+
+        def issue(t, u):
+            h, o, _ = place_of(t // 4)
+            for unit in range(2):
+                pltpu.matmul_push_rhs(right[2 * u + unit], u % 2, unit)
+                for n in range(2):
+                    feed(unit, 4 * (u % 2) + 2 * n, got[h, o + n], u % 2 if n == 0 else None)
+
+        def drain(t, u):
+            h, o, to = place_of(t // 4)
+            if u == 0:
+                put(full, h, to, got[h, o, :64].astype(F32), got[h, o + 1, :64].astype(F32), 0)
+                put(full, h, to, got[h, o, 64:].astype(F32), got[h, o + 1, 64:].astype(F32), 8)
+            for unit in range(2):
+                mine = acc[unit][4 * (u % 2) : 4 * (u % 2) + 4]
+                for n in range(2):
+                    put(image.at[2 * u + unit], h, to, pltpu.matmul_pop(mine[n]), pltpu.matmul_pop(mine[2 + n]), 8 * n)
+
+        in_turns(4 * count, issue, drain, 4)
 
     for h in range(2):
         for dp, half, sp in ((3, 0, 1), (1, 1, -1)):
@@ -177,26 +202,26 @@
     def source(k, s):
         return lax.rem(src_ref[k, s], 32)
 
-    def sigma_of(s, unit, buf):
-        for t in range(4):
-            rhs = jnp.concatenate([image[k, source(k, s)] for k in (2 * t, 2 * t + 1)], axis=0)
-            lhs = jnp.concatenate([scaled[2 * t, s], scaled[2 * t + 1, s]], axis=1)
-            pltpu.matmul_push_rhs(rhs, t % 2, unit)
-            pltpu.matmul_acc_lhs(acc[unit][buf], lhs, t % 2)
-
     def sigma_chunk(c):
-        @pl.loop(c * (8 // CHUNKS), (c + 1) * (8 // CHUNKS))
-        def _(i):
-            for pair in range(2):
-                at_pair = 2 * i + pair
+        def issue(t, u):
+            for t2 in range(4):
                 for e in range(2):
-                    sigma_of(2 * at_pair + e, e, pair)
-                first, second = pltpu.matmul_pop(acc[0][pair]), pltpu.matmul_pop(acc[1][pair])
-                rows = pl.ds(pl.multiple_of(at_pair * 16, 16), 16)
-                for o in range(16):
+                    s = 2 * (c * (16 // CHUNKS) + t) + e
+                    rhs = jnp.concatenate([image[k, source(k, s)] for k in (2 * t2, 2 * t2 + 1)], axis=0)
+                    lhs = jnp.concatenate([scaled[2 * t2, s], scaled[2 * t2 + 1, s]], axis=1)
+                    pltpu.matmul_push_rhs(rhs, t2 % 2, e)
+                    feed(e, 2 * (u % 2), lhs, t2 % 2)
+
+        def drain(t, u):
+            rows = pl.ds(pl.multiple_of((c * (16 // CHUNKS) + t) * 16, 16), 16)
+            for n in range(2):
+                first, second = pltpu.matmul_pop(acc[0][2 * (u % 2) + n]), pltpu.matmul_pop(acc[1][2 * (u % 2) + n])
+                for o in range(8):
                     two = jnp.concatenate([first[o * 8 : o * 8 + 8], second[o * 8 : o * 8 + 8]], axis=0).astype(BF16)
-                    parts[0, o // 4, o % 4, rows, :] = two[:, :128]
-                    parts[1, o % 4, o // 4, rows, :] = two[:, 128:]
+                    parts[0, 2 * n + o // 4, o % 4, rows, :] = two[:, :128]
+                    parts[1, o % 4, 2 * n + o // 4, rows, :] = two[:, 128:]
+
+        in_turns(16 // CHUNKS, issue, drain, 4)
 
     steps = ((0, 1), (1, 3))
 
@@ -250,41 +275,38 @@
             sig_ref[rows, pl.ds(h * 128, 128)] = total * (128 ** -0.5)
 
     def mix(ks, turning=False):
-        @pl.loop(0, 4)
+        none = jnp.zeros((128, 128), BF16)
+
+        def issue(t, u):
+            for j in range(2):
+                rhs = jnp.concatenate([full[source(ks[j], 2 * t + n)] for n in range(2)], axis=0)
+                pltpu.matmul_push_rhs(rhs, u % 2, j)
+                for n in range(2):
+                    one = left[ks[j], 2 * t + n]
+                    lhs = jnp.concatenate([one, none] if n == 0 else [none, one], axis=1)
+                    feed(j, 4 * (u % 2) + 2 * n, lhs, u % 2 if n == 0 else None)
+
+        def drain(t, u):
+            if turning:
+                for n in range(2):
+                    full_t[t, :, n * 128 : n * 128 + 128] = full[2 * t + n].T
+            for j in range(2):
+                for n in range(4):
+                    zed[j, t, n * 64 : n * 64 + 64, :] = pltpu.matmul_pop(acc[j][4 * (u % 2) + n]).astype(BF16)
+
+        in_turns(16, issue, drain, 4)
+
+    def renorm(slot):
+        @pl.loop(0, 2)
         def _(i):
-            none = jnp.zeros((128, 128), BF16)
-            for e in range(4):
-                at_pair = 4 * i + e
-                if turning:
-                    for n in range(2):
-                        full_t[at_pair, :, n * 128 : n * 128 + 128] = full[2 * at_pair + n].T
+            for e in range(8):
                 for j in range(2):
-                    rhs = jnp.concatenate([full[source(ks[j], 2 * at_pair + n)] for n in range(2)], axis=0)
-                    pltpu.matmul_push_rhs(rhs, e % 2, j)
-                    for n in range(2):
-                        one = left[ks[j], 2 * at_pair + n]
-                        lhs = jnp.concatenate([one, none] if n == 0 else [none, one], axis=1)
-                        pltpu.matmul_acc_lhs(acc[j][e % 2 * 2 + n], lhs, e % 2 if n == 0 else None)
-                for j in range(2):
-                    for n in range(2):
-                        zed[j, at_pair, n * 128 : n * 128 + 128, :] = pltpu.matmul_pop(acc[j][e % 2 * 2 + n]).astype(BF16)
-
-    def renorm(slot):
-        @pl.loop(0, 4)
-        def _(i):
-            for e in range(4):
-                for j in range(2):
-                    pltpu.matmul_push_rhs(zed[j, 4 * i + e], e % 2, j)
-                    for half in range(2):
-                        pltpu.matmul_acc_lhs(
-                            acc[j][half], full_t[4 * i + e, half * 128 : half * 128 + 128, :], e % 2 if half == 0 else None
-                        )
+                    pltpu.matmul_push_rhs(zed[j, 8 * i + e], e % 2, j)
+                    feed(j, 0, full_t[8 * i + e], e % 2)
 
         for j in range(2):
-            for half in range(2):
-                block[slot + j, half * 128 : half * 128 + 128, :] = (
-                    pltpu.matmul_pop(acc[j][half]) * (4096 ** -0.5)
-                ).astype(BF16)
+            for n in range(4):
+                block[slot + j, n * 64 : n * 64 + 64, :] = (pltpu.matmul_pop(acc[j][n]) * (4096 ** -0.5)).astype(BF16)
 
     def push(src, dst, kind, recv_sem, target):
         pltpu.make_async_remote_copy(
@@ -361,7 +383,7 @@
 
 
 def with_totals(*refs):
-    totals = [pltpu.ACC(unit)((128, 256), F32) for unit in (0, 0, 0, 0, 1, 1, 1, 1)]
+    totals = [pltpu.ACC(unit)((64, 256), F32) for unit in range(2) for _ in range(8)]
     pl.run_scoped(functools.partial(kernel, *refs), *totals)
 
 

time: 55.3 us -> 54.4 us (0.984)
  Pallas kernels: 54.4 us -> 53.6 us
    pallas_call x1, Pallas kernels: 51.9 us -> 51.2 us  [body(): pl.pallas_call(with_totals, out_shape=(jax.ShapeDtypeStruct((256, 256), F...]
where the time goes in v4:
time: 54.4 us; the launch traced here: 54.2 us
  Pallas kernels  53.6 us (99%)
  between operations  0.64 us (1%)
    pallas_call x1, Pallas kernels, body(): pl.pallas_call(with_totals, out_shape=(jax.ShapeDtypeStruct((256, 256), F...  51.2 us
    pallas_call x1, Pallas kernels, body(): pl.pallas_call(finish, out_shape=(jax.ShapeDtypeStruct((256, 256), BF16),...  2.42 us

profile of v4, /device:TPU:0, one launch (start us, length us, event | category | flops | bytes accessed | tf_op | source)
XLA Modules:
  0.0 54.2 jit_solution(15165299726897458998)
XLA Ops:
  0.6 51.2 %dmrg_step.1 = (f32[256,256]{1,0:T(8,128)}, bf16[8,256,256]{2,1,0:T(8,128)(2,1)}) custom-call(bf16[256,256]{1,0:T(8,128)(2,1)} %bitcast.6, bf16[8,32,128,128]{3,2,1,0:T(8,128)(2,1)} %refs_1_.1, bf16[8,256,256]{2,1,0:T(8,128)(2,1)} %bitcast.5, s32[8,32]{1,0:T(8,128)} %refs_3_.1, s32[8,32]{1,0:T(8,128)} %refs_4_.1), custom_call_target="tpu_custom_call" | custom-call | flops 12999999488 | bytes 12582912 | tf_op jit(solution)/shard_map/dmrg_step/pallas_call | solution.py:411
  51.8 2.4 %finish.1 = (bf16[256,256]{1,0:T(8,128)(2,1)}, f32[8,256,256]{2,1,0:T(8,128)}) custom-call(f32[256,256]{1,0:T(8,128)} %get-tuple-element.6.sig_ref, bf16[8,256,256]{2,1,0:T(8,128)(2,1)} %get-tuple-element.7.ren_ref), custom_call_target="tpu_custom_call" | custom-call | tf_op jit(solution)/shard_map/finish/pallas_call | solution.py:448

commit v5 on v4

--- a/solution.py
+++ b/solution.py
@@ -11,7 +11,8 @@
 MESH = pl.DeviceIdType.MESH
 F32 = jnp.float32
 BF16 = jnp.bfloat16
-CHUNKS = 2
+CUTS = (0, 8, 20, 32)
+CHUNKS = len(CUTS) - 1
 
 
 def turn(a, step):
@@ -19,11 +20,11 @@
 
 
 def kernel(
-    psi_ref, left_ref, right_ref, src_ref, cpl_ref,
-    sig_ref, ren_ref,
-    left, scaled, right, got, full, full_t, image, zed, parts, block,
+    psi_ref, left_ref, right_ref, src_hbm, cpl_hbm,
+    sig_out, ren_ref,
+    src_ref, cpl_ref, sig_ref, left, scaled, right, got, full, full_t, image, zed, parts, block,
     hop1, hop2, kept, hop3, hop4, relay,
-    load_sem, send_sem, gather_sem, sum_sem, swap_sem, relay_sem, far_sem, own_sem,
+    load_sem, send_sem, gather_sem, sum_sem, swap_sem, relay_sem, far_sem, own_sem, leave_sem,
     *totals,
 ):
     acc = (totals[:8], totals[8:])
@@ -32,19 +33,20 @@
     y, core = sec // 2, sec % 2
     coords = ((x, z), (z, x))
 
+    barrier = pltpu.get_barrier_semaphore()
+    peers = [(z * 4 + turn(x, 1), sec), (z * 4 + turn(x, 3), sec), (turn(z, 1) * 4 + x, sec), (turn(z, 3) * 4 + x, sec)]
+    peers += [(op, lax.rem(sec + i, 8)) for i in range(1, 8)]
+    for peer in peers:
+        pl.semaphore_signal(barrier, inc=1, device_id=peer, device_id_type=MESH)
     loads = [
         pltpu.make_async_copy(psi_ref.at[pl.ds(h * 128, 128)], got.at[h, op], load_sem.at[h]) for h in range(2)
     ]
     loads.append(pltpu.make_async_copy(right_ref, right, load_sem.at[2]))
     loads += [pltpu.make_async_copy(left_ref.at[k], left.at[k], load_sem.at[3 + k]) for k in range(8)]
-    for copy in loads:
+    loads.append(pltpu.make_async_copy(cpl_hbm, cpl_ref, load_sem.at[11]))
+    loads.append(pltpu.make_async_copy(src_hbm, src_ref, load_sem.at[12]))
+    for copy in loads[:2] + loads[11:] + loads[2:11]:
         copy.start()
-
-    barrier = pltpu.get_barrier_semaphore()
-    peers = [(z * 4 + turn(x, 1), sec), (z * 4 + turn(x, 3), sec), (turn(z, 1) * 4 + x, sec), (turn(z, 3) * 4 + x, sec)]
-    peers += [(op, lax.rem(sec + i, 8)) for i in range(1, 8)]
-    for peer in peers:
-        pl.semaphore_signal(barrier, inc=1, device_id=peer, device_id_type=MESH)
     pl.semaphore_wait(barrier, len(peers))
 
     def place(h, p, q):
@@ -119,85 +121,106 @@
                 issue(t + 1, u + 1)
             drain(t, u)
 
-    def images(count, which):
-        def place_of(i):
-            h, dz, other = which(i)
-            j = x // 2
-            j = j + other * (1 - 2 * j)
-            zz = lax.rem(z + dz, 4)
-            return h, zz * 4 + 2 * j, pl.ds(pl.multiple_of(zz * 32 + j * 16, 16), 16)
-
-        def put(ref, h, to, first, second, at_sector):
+    waiting = []
+
+    def unit_image(h, dz, other):
+        j = x // 2
+        if other:
+            j = 1 - j
+        zz = turn(z, dz)
+        o, to = zz * 4 + 2 * j, pl.ds(pl.multiple_of(zz * 32 + j * 16, 16), 16)
+
+        def put(ref, first, second, at_sector):
             for s in range(8):
                 two = jnp.concatenate([first[s * 8 : s * 8 + 8], second[s * 8 : s * 8 + 8]], axis=0)
                 ref[h * 16 + at_sector + s, to, :] = two.astype(BF16)
 
-        def issue(t, u):
-            h, o, _ = place_of(t // 4)
+        def drain(u):
+            if u == 0:
+                put(full, got[h, o, :64].astype(F32), got[h, o + 1, :64].astype(F32), 0)
+                put(full, got[h, o, 64:].astype(F32), got[h, o + 1, 64:].astype(F32), 8)
+            for unit in range(2):
+                mine = acc[unit][4 * (u % 2) : 4 * (u % 2) + 4]
+                for n in range(2):
+                    put(image.at[2 * u + unit], pltpu.matmul_pop(mine[n]), pltpu.matmul_pop(mine[2 + n]), 8 * n)
+
+        for u in range(4):
             for unit in range(2):
                 pltpu.matmul_push_rhs(right[2 * u + unit], u % 2, unit)
                 for n in range(2):
                     feed(unit, 4 * (u % 2) + 2 * n, got[h, o + n], u % 2 if n == 0 else None)
-
-        def drain(t, u):
-            h, o, to = place_of(t // 4)
-            if u == 0:
-                put(full, h, to, got[h, o, :64].astype(F32), got[h, o + 1, :64].astype(F32), 0)
-                put(full, h, to, got[h, o, 64:].astype(F32), got[h, o + 1, 64:].astype(F32), 8)
-            for unit in range(2):
-                mine = acc[unit][4 * (u % 2) : 4 * (u % 2) + 4]
-                for n in range(2):
-                    put(image.at[2 * u + unit], h, to, pltpu.matmul_pop(mine[n]), pltpu.matmul_pop(mine[2 + n]), 8 * n)
-
-        in_turns(4 * count, issue, drain, 4)
-
-    for h in range(2):
-        for dp, half, sp in ((3, 0, 1), (1, 1, -1)):
+            if waiting:
+                waiting.pop()()
+            waiting.append(functools.partial(drain, u))
+
+    both_ways = ((3, 0, 1), (1, 1, -1))
+
+    def from_p(h):
+        for dp, half, sp in both_ways:
             await_piece(h, dp, 0, None)
             pass_on(h, dp, 0, half, sp, 0)
             for sq in (1, -1):
                 pass_on(h, dp, 0, None, 0, sq)
-    for h in range(2):
-        for dq, half, sq in ((3, 0, 1), (1, 1, -1)):
-            await_piece(h, 0, dq, None)
-            pass_on(h, 0, dq, half, 0, sq)
-    loads[2].wait()
-    images(2, lambda i: (i, 0, 0))
-    scale(0)
-    for h in range(2):
-        await_piece(h, 2, 0, 0)
-        await_piece(h, 2, 0, 1)
+
+    def from_p2(h):
+        for half in range(2):
+            await_piece(h, 2, 0, half)
         for sq in (1, -1):
             pass_on(h, 2, 0, None, 0, sq)
+
+    def from_q(h, dp):
+        for dq, half, sq in both_ways:
+            await_piece(h, dp, dq, None)
+            pass_on(h, dp, dq, half, 0, sq)
+
+    def from_q2(h, dp):
+        for half in range(2):
+            await_piece(h, dp, 2, half)
+
+    loads[11].wait()
+    loads[12].wait()
+    scale(0)
+    from_p(0)
+    from_p(1)
     scale(1)
-    for h in range(2):
-        await_piece(h, 0, 2, 0)
-        await_piece(h, 0, 2, 1)
-    images(2, lambda i: (i, 0, 1))
+    from_q(0, 0)
+    from_q(1, 0)
+    loads[2].wait()
+    unit_image(0, 0, 0)
+    unit_image(1, 0, 0)
+    from_p2(0)
+    from_p2(1)
+    unit_image(0, 0, 1)
+    from_q2(0, 0)
+    from_q2(1, 0)
+    unit_image(1, 0, 1)
     scale(2)
-    for h in range(2):
-        for dp in (3, 1):
-            for dq, half, sq in ((3, 0, 1), (1, 1, -1)):
-                await_piece(h, dp, dq, None)
-                pass_on(h, dp, dq, half, 0, sq)
-    images(4, lambda i: (i // 2, 3 + 2 * (i % 2), 0))
-    for h in range(2):
-        for dq, half, sq in ((3, 0, 1), (1, 1, -1)):
-            await_piece(h, 2, dq, None)
-            pass_on(h, 2, dq, half, 0, sq)
+    from_q(0, 3)
+    from_q(1, 3)
     scale(3)
-    images(3, lambda i: (i // 2, 3 + 2 * i + 3 * (i // 2), 1 - i // 2))
-    for h in range(2):
-        for dp in (3, 1):
-            for half in range(2):
-                await_piece(h, dp, 2, half)
-    images(3, lambda i: (1 - i // 2, 3 + 2 * i + 3 * (i // 2), 1 - i // 2))
-    for h in range(2):
-        for half in range(2):
-            await_piece(h, 2, 2, half)
-    images(2, lambda i: (i, 2, 1))
-
-    span = 32 // CHUNKS * 8
+    from_q(0, 1)
+    from_q(1, 1)
+    unit_image(0, 3, 0)
+    unit_image(1, 3, 0)
+    unit_image(0, 1, 0)
+    unit_image(1, 1, 0)
+    from_q(0, 2)
+    from_q(1, 2)
+    unit_image(0, 3, 1)
+    unit_image(0, 1, 1)
+    unit_image(1, 2, 0)
+    from_q2(0, 3)
+    from_q2(0, 1)
+    unit_image(0, 2, 0)
+    from_q2(1, 3)
+    unit_image(1, 3, 1)
+    from_q2(1, 1)
+    unit_image(1, 1, 1)
+    from_q2(0, 2)
+    unit_image(0, 2, 1)
+    from_q2(1, 2)
+    unit_image(1, 2, 1)
+    waiting.pop()()
 
     def source(k, s):
         return lax.rem(src_ref[k, s], 32)
@@ -206,14 +229,14 @@
         def issue(t, u):
             for t2 in range(4):
                 for e in range(2):
-                    s = 2 * (c * (16 // CHUNKS) + t) + e
+                    s = CUTS[c] + 2 * t + e
                     rhs = jnp.concatenate([image[k, source(k, s)] for k in (2 * t2, 2 * t2 + 1)], axis=0)
                     lhs = jnp.concatenate([scaled[2 * t2, s], scaled[2 * t2 + 1, s]], axis=1)
                     pltpu.matmul_push_rhs(rhs, t2 % 2, e)
                     feed(e, 2 * (u % 2), lhs, t2 % 2)
 
         def drain(t, u):
-            rows = pl.ds(pl.multiple_of((c * (16 // CHUNKS) + t) * 16, 16), 16)
+            rows = pl.ds(pl.multiple_of(CUTS[c] * 8 + t * 16, 16), 16)
             for n in range(2):
                 first, second = pltpu.matmul_pop(acc[0][2 * (u % 2) + n]), pltpu.matmul_pop(acc[1][2 * (u % 2) + n])
                 for o in range(8):
@@ -221,58 +244,82 @@
                     parts[0, 2 * n + o // 4, o % 4, rows, :] = two[:, :128]
                     parts[1, o % 4, 2 * n + o // 4, rows, :] = two[:, 128:]
 
-        in_turns(16 // CHUNKS, issue, drain, 4)
+        in_turns((CUTS[c + 1] - CUTS[c]) // 2, issue, drain, 2)
 
     steps = ((0, 1), (1, 3))
 
-    def rows_of(c, half):
-        return pl.ds(c * span + half * (span // 2), span // 2)
+    def all_rows(c):
+        return pl.ds(CUTS[c] * 8, (CUTS[c + 1] - CUTS[c]) * 8)
+
+    def half_of(c, d):
+        span = (CUTS[c + 1] - CUTS[c]) * 4
+        return pl.ds(CUTS[c] * 8 + d * span, span)
+
+    def small(c):
+        return pl.ds(CUTS[c] * 4, (CUTS[c + 1] - CUTS[c]) * 4)
 
     def sum1(c):
         for h in range(2):
             p, q = coords[h]
             for d, step in steps:
-                start(parts.at[h, turn(q, 2), :, rows_of(c, d), :], hop1.at[h, d, c], 2, sum_sem.at[0, h, d, c], at(h, 0, step))
+                start(
+                    parts.at[h, turn(q, 2), :, half_of(c, d), :], hop1.at[h, d, :, small(c), :],
+                    2, sum_sem.at[0, h, d, c], at(h, 0, step),
+                )
 
     def sum2(c):
         for h in range(2):
             p, q = coords[h]
             for d, step in steps:
-                arrived(hop1.at[h, d, c], sum_sem.at[0, h, d, c])
+                arrived(hop1.at[h, d, :, small(c), :], sum_sem.at[0, h, d, c])
                 near = turn(q, step)
-                old = parts[h, near, :, rows_of(c, d), :].astype(F32)
-                parts[h, near, :, rows_of(c, d), :] = (old + hop1[h, d, c].astype(F32)).astype(BF16)
-                start(parts.at[h, near, :, pl.ds(c * span, span), :], hop2.at[h, d, c], 3, sum_sem.at[1, h, d, c], at(h, 0, step))
+                old = parts[h, near, :, half_of(c, d), :].astype(F32)
+                parts[h, near, :, half_of(c, d), :] = (old + hop1[h, d, :, small(c), :].astype(F32)).astype(BF16)
+                start(
+                    parts.at[h, near, :, all_rows(c), :], hop2.at[h, d, :, all_rows(c), :],
+                    3, sum_sem.at[1, h, d, c], at(h, 0, step),
+                )
 
     def sum3(c):
         for h in range(2):
             p, q = coords[h]
-            for d, step in steps:
-                arrived(hop2.at[h, d, c], sum_sem.at[1, h, d, c])
-            rows = pl.ds(c * span, span)
-            total = parts[h, q, :, rows, :].astype(F32) + hop2[h, 0, c].astype(F32) + hop2[h, 1, c].astype(F32)
+            rows = all_rows(c)
+            for d, step in steps:
+                arrived(hop2.at[h, d, :, rows, :], sum_sem.at[1, h, d, c])
+            total = parts[h, q, :, rows, :].astype(F32)
+            total = total + hop2[h, 0, :, rows, :].astype(F32) + hop2[h, 1, :, rows, :].astype(F32)
             kept[h, :, rows, :] = total.astype(BF16)
             for d, step in steps:
-                start(kept.at[h, turn(p, 2), rows_of(c, d), :], hop3.at[h, d, c], 4, sum_sem.at[2, h, d, c], at(h, step, 0))
+                start(
+                    kept.at[h, turn(p, 2), half_of(c, d), :], hop3.at[h, d, small(c), :],
+                    4, sum_sem.at[2, h, d, c], at(h, step, 0),
+                )
 
     def sum4(c):
         for h in range(2):
             p, q = coords[h]
             for d, step in steps:
-                arrived(hop3.at[h, d, c], sum_sem.at[2, h, d, c])
+                arrived(hop3.at[h, d, small(c), :], sum_sem.at[2, h, d, c])
                 near = turn(p, step)
-                old = kept[h, near, rows_of(c, d), :].astype(F32)
-                kept[h, near, rows_of(c, d), :] = (old + hop3[h, d, c].astype(F32)).astype(BF16)
-                start(kept.at[h, near, pl.ds(c * span, span), :], hop4.at[h, d, c], 5, sum_sem.at[3, h, d, c], at(h, step, 0))
+                old = kept[h, near, half_of(c, d), :].astype(F32)
+                kept[h, near, half_of(c, d), :] = (old + hop3[h, d, small(c), :].astype(F32)).astype(BF16)
+                start(
+                    kept.at[h, near, all_rows(c), :], hop4.at[h, d, all_rows(c), :],
+                    5, sum_sem.at[3, h, d, c], at(h, step, 0),
+                )
+
+    leaves = []
 
     def sum5(c):
+        rows = all_rows(c)
         for h in range(2):
             p, q = coords[h]
             for d, step in steps:
-                arrived(hop4.at[h, d, c], sum_sem.at[3, h, d, c])
-            rows = pl.ds(c * span, span)
-            total = kept[h, p, rows, :].astype(F32) + hop4[h, 0, c].astype(F32) + hop4[h, 1, c].astype(F32)
+                arrived(hop4.at[h, d, rows, :], sum_sem.at[3, h, d, c])
+            total = kept[h, p, rows, :].astype(F32) + hop4[h, 0, rows, :].astype(F32) + hop4[h, 1, rows, :].astype(F32)
             sig_ref[rows, pl.ds(h * 128, 128)] = total * (128 ** -0.5)
+        leaves.append(pltpu.make_async_copy(sig_ref.at[rows, :], sig_out.at[rows, :], leave_sem.at[c]))
+        leaves[-1].start()
 
     def mix(ks, turning=False):
         none = jnp.zeros((128, 128), BF16)
@@ -342,33 +389,39 @@
 
     sigma_chunk(0)
     sum1(0)
+    mix(far, turning=True)
+    renorm(0)
+    ship_far()
+    sum2(0)
     sigma_chunk(1)
     sum1(1)
-    mix(far, turning=True)
-    sum2(0)
-    renorm(0)
-    ship_far()
+    sigma_chunk(2)
+    sum1(2)
+    sum3(0)
+    mix(near[0])
+    relay_far()
     sum2(1)
-    mix(near[0])
-    sum3(0)
     renorm(2)
     ship(2, 1, near[0][0])
     ship(3, 3, near[0][1])
-    relay_far()
+    sum2(2)
     sum4(0)
     mix(near[1])
-    sum3(1)
     renorm(4)
     ship(4, 1, near[1][0])
     ship(5, 3, near[1][1])
+    sum3(1)
     sum5(0)
     mix(here)
+    sum3(2)
     sum4(1)
     renorm(6)
     ship(7 - core, 0, 2 * y + 1 - core)
     own = pltpu.make_async_copy(block.at[6 + core], ren_ref.at[sec], own_sem)
     own.start()
+    sum4(2)
     sum5(1)
+    sum5(2)
     for dy in (1, 3):
         for c in range(2):
             swapped(dy, c)
@@ -377,6 +430,8 @@
             arrived(ren_ref.at[turn(y, 2) * 2 + c, half_rows(d)], far_sem.at[d, c])
     swapped(0, 1 - core)
     own.wait()
+    for copy in leaves:
+        copy.wait()
     all_sent = (got.at[0, pl.ds(0, 15)], got.at[1, pl.ds(0, 15)], hop1, hop2, hop3, hop4, block.at[pl.ds(0, 7)], relay)
     for kind, ref in enumerate(all_sent):
         pltpu.make_async_copy(ref, ref, send_sem.at[kind]).wait()
@@ -407,13 +462,15 @@
 
 def body(psi, left_env, right_env, source, coupling):
     vm = pltpu.VMEM
-    rows = 256 // CHUNKS
     sig, ren = pl.pallas_call(
         with_totals,
         out_shape=(jax.ShapeDtypeStruct((256, 256), F32), jax.ShapeDtypeStruct((8, 256, 256), BF16)),
-        in_specs=[pl.BlockSpec(memory_space=pl.ANY)] * 3 + [pl.BlockSpec(memory_space=pltpu.SMEM)] * 2,
-        out_specs=(pl.BlockSpec(memory_space=pltpu.VMEM), pl.BlockSpec(memory_space=pl.ANY)),
+        in_specs=[pl.BlockSpec(memory_space=pl.ANY)] * 5,
+        out_specs=(pl.BlockSpec(memory_space=pl.ANY), pl.BlockSpec(memory_space=pl.ANY)),
         scratch_shapes=[
+            pltpu.SMEM((8, 32), jnp.int32),
+            pltpu.SMEM((8, 32), jnp.int32),
+            vm((256, 256), F32),
             vm((8, 32, 128, 128), BF16),
             vm((8, 32, 128, 128), BF16),
             vm((8, 256, 256), BF16),
@@ -424,13 +481,13 @@
             vm((2, 16, 256, 256), BF16),
             vm((2, 4, 4, 256, 128), BF16),
             vm((8, 256, 256), BF16),
-            vm((2, 2, CHUNKS, 4, rows // 2, 128), BF16),
-            vm((2, 2, CHUNKS, 4, rows, 128), BF16),
+            vm((2, 2, 4, 128, 128), BF16),
+            vm((2, 2, 4, 256, 128), BF16),
             vm((2, 4, 256, 128), BF16),
-            vm((2, 2, CHUNKS, rows // 2, 128), BF16),
-            vm((2, 2, CHUNKS, rows, 128), BF16),
+            vm((2, 2, 128, 128), BF16),
+            vm((2, 2, 256, 128), BF16),
             vm((2, 2, 128, 256), BF16),
-            pltpu.SemaphoreType.DMA((11,)),
+            pltpu.SemaphoreType.DMA((13,)),
             pltpu.SemaphoreType.DMA((8,)),
             pltpu.SemaphoreType.DMA((2, 16, 2)),
             pltpu.SemaphoreType.DMA((4, 2, 2, CHUNKS)),
@@ -438,6 +495,7 @@
             pltpu.SemaphoreType.DMA((2, 2)),
             pltpu.SemaphoreType.DMA((2, 2)),
             pltpu.SemaphoreType.DMA,
+            pltpu.SemaphoreType.DMA((CHUNKS,)),
         ],
         compiler_params=pltpu.CompilerParams(
             collective_id=0, has_side_effects=True, vmem_limit_bytes=60 * 1024 * 1024

time: 54.4 us -> 54.7 us (level)
  no operation moved by 1% of the time
where the time goes in v5:
time: 54.7 us; the launch traced here: 54.5 us
  Pallas kernels  53.9 us (99%)
  between operations  0.64 us (1%)
    pallas_call x1, Pallas kernels, body(): pl.pallas_call(with_totals, out_shape=(jax.ShapeDtypeStruct((256, 256), F...  51.5 us
    pallas_call x1, Pallas kernels, body(): pl.pallas_call(finish, out_shape=(jax.ShapeDtypeStruct((256, 256), BF16),...  2.42 us

profile of v5, /device:TPU:0, one launch (start us, length us, event | category | flops | bytes accessed | tf_op | source)
XLA Modules:
  0.0 54.5 jit_solution(14581728013087591350)
XLA Ops:
  0.6 51.5 %dmrg_step.1 = (f32[256,256]{1,0:T(8,128)}, bf16[8,256,256]{2,1,0:T(8,128)(2,1)}) custom-call(bf16[256,256]{1,0:T(8,128)(2,1)} %bitcast.6, bf16[8,32,128,128]{3,2,1,0:T(8,128)(2,1)} %refs_1_.1, bf16[8,256,256]{2,1,0:T(8,128)(2,1)} %bitcast.5, s32[8,32]{1,0:T(8,128)} %refs_3_.1, s32[8,32]{1,0:T(8,128)} %refs_4_.1), custom_call_target="tpu_custom_call" | custom-call | flops 12999999488 | bytes 12582912 | tf_op jit(solution)/shard_map/dmrg_step/pallas_call | solution.py:465
  52.1 2.4 %finish.1 = (bf16[256,256]{1,0:T(8,128)(2,1)}, f32[8,256,256]{2,1,0:T(8,128)}) custom-call(f32[256,256]{1,0:T(8,128)} %get-tuple-element.6.sig_ref, bf16[8,256,256]{2,1,0:T(8,128)(2,1)} %get-tuple-element.7.ren_ref), custom_call_target="tpu_custom_call" | custom-call | tf_op jit(solution)/shard_map/finish/pallas_call | solution.py:506

commit v6 on v5

--- a/solution.py
+++ b/solution.py
@@ -31,7 +31,12 @@
     op, sec = lax.axis_index("op"), lax.axis_index("sec")
     z, x = op // 4, op % 4
     y, core = sec // 2, sec % 2
-    coords = ((x, z), (z, x))
+    flows = (core, 1 - core)
+    coords = tuple((x + f * (z - x), z + f * (x - z)) for f in flows)
+
+    def step_of(a, step):
+        return lax.rem(a + (1 + 2 * core) * (step % 4), 4)
+
 
     barrier = pltpu.get_barrier_semaphore()
     peers = [(z * 4 + turn(x, 1), sec), (z * 4 + turn(x, 3), sec), (turn(z, 1) * 4 + x, sec), (turn(z, 3) * 4 + x, sec)]
@@ -50,11 +55,11 @@
     pl.semaphore_wait(barrier, len(peers))
 
     def place(h, p, q):
-        return q * 4 + p if h == 0 else p * 4 + q
+        return q * 4 + p + flows[h] * (3 * p - 3 * q)
 
     def at(h, dp, dq):
         p, q = coords[h]
-        return place(h, turn(p, dp), turn(q, dq))
+        return place(h, step_of(p, dp), step_of(q, dq))
 
     def start(src, dst, kind, recv_sem, target):
         pltpu.make_async_remote_copy(
@@ -69,7 +74,7 @@
         ).wait_recv()
 
     def piece(h, dp, dq, half):
-        ref = got.at[h, at(h, dp, dq)]
+        ref = got.at[flows[h], at(h, dp, dq)]
         return ref if half is None else ref.at[pl.ds(half * 64, 64)]
 
     def pass_on(h, dp, dq, half, sp, sq):
@@ -80,8 +85,9 @@
     def await_piece(h, dp, dq, half):
         arrived(piece(h, dp, dq, half), gather_sem.at[h, dp * 4 + dq, 0 if half is None else half])
 
+    loads[0].wait()
+    loads[1].wait()
     for h in range(2):
-        loads[h].wait()
         for sp in (1, -1):
             pass_on(h, 0, 0, None, sp, 0)
     for h in range(2):
@@ -127,7 +133,7 @@
         j = x // 2
         if other:
             j = 1 - j
-        zz = turn(z, dz)
+        zz = step_of(z, dz)
         o, to = zz * 4 + 2 * j, pl.ds(pl.multiple_of(zz * 32 + j * 16, 16), 16)
 
         def put(ref, first, second, at_sector):
@@ -209,16 +215,15 @@
     unit_image(0, 3, 1)
     unit_image(0, 1, 1)
     unit_image(1, 2, 0)
-    from_q2(0, 3)
-    from_q2(0, 1)
+    for h in range(2):
+        from_q2(h, 3)
+        from_q2(h, 1)
     unit_image(0, 2, 0)
-    from_q2(1, 3)
     unit_image(1, 3, 1)
-    from_q2(1, 1)
     unit_image(1, 1, 1)
     from_q2(0, 2)
+    from_q2(1, 2)
     unit_image(0, 2, 1)
-    from_q2(1, 2)
     unit_image(1, 2, 1)
     waiting.pop()()
 
@@ -263,7 +268,7 @@
             p, q = coords[h]
             for d, step in steps:
                 start(
-                    parts.at[h, turn(q, 2), :, half_of(c, d), :], hop1.at[h, d, :, small(c), :],
+                    parts.at[flows[h], turn(q, 2), :, half_of(c, d), :], hop1.at[h, d, :, small(c), :],
                     2, sum_sem.at[0, h, d, c], at(h, 0, step),
                 )
 
@@ -272,11 +277,11 @@
             p, q = coords[h]
             for d, step in steps:
                 arrived(hop1.at[h, d, :, small(c), :], sum_sem.at[0, h, d, c])
-                near = turn(q, step)
-                old = parts[h, near, :, half_of(c, d), :].astype(F32)
-                parts[h, near, :, half_of(c, d), :] = (old + hop1[h, d, :, small(c), :].astype(F32)).astype(BF16)
+                near = step_of(q, step)
+                old = parts[flows[h], near, :, half_of(c, d), :].astype(F32)
+                parts[flows[h], near, :, half_of(c, d), :] = (old + hop1[h, d, :, small(c), :].astype(F32)).astype(BF16)
                 start(
-                    parts.at[h, near, :, all_rows(c), :], hop2.at[h, d, :, all_rows(c), :],
+                    parts.at[flows[h], near, :, all_rows(c), :], hop2.at[h, d, :, all_rows(c), :],
                     3, sum_sem.at[1, h, d, c], at(h, 0, step),
                 )
 
@@ -286,7 +291,7 @@
             rows = all_rows(c)
             for d, step in steps:
                 arrived(hop2.at[h, d, :, rows, :], sum_sem.at[1, h, d, c])
-            total = parts[h, q, :, rows, :].astype(F32)
+            total = parts[flows[h], q, :, rows, :].astype(F32)
             total = total + hop2[h, 0, :, rows, :].astype(F32) + hop2[h, 1, :, rows, :].astype(F32)
             kept[h, :, rows, :] = total.astype(BF16)
             for d, step in steps:
@@ -300,7 +305,7 @@
             p, q = coords[h]
             for d, step in steps:
                 arrived(hop3.at[h, d, small(c), :], sum_sem.at[2, h, d, c])
-                near = turn(p, step)
+                near = step_of(p, step)
                 old = kept[h, near, half_of(c, d), :].astype(F32)
                 kept[h, near, half_of(c, d), :] = (old + hop3[h, d, small(c), :].astype(F32)).astype(BF16)
                 start(
@@ -317,7 +322,7 @@
             for d, step in steps:
                 arrived(hop4.at[h, d, rows, :], sum_sem.at[3, h, d, c])
             total = kept[h, p, rows, :].astype(F32) + hop4[h, 0, rows, :].astype(F32) + hop4[h, 1, rows, :].astype(F32)
-            sig_ref[rows, pl.ds(h * 128, 128)] = total * (128 ** -0.5)
+            sig_ref[rows, pl.ds(pl.multiple_of(flows[h] * 128, 128), 128)] = total * (128 ** -0.5)
         leaves.append(pltpu.make_async_copy(sig_ref.at[rows, :], sig_out.at[rows, :], leave_sem.at[c]))
         leaves[-1].start()
 
@@ -362,7 +367,7 @@
         ).start()
 
     def ship(slot, dy, target):
-        push(block.at[slot], ren_ref.at[sec], 6, swap_sem.at[dy, core], target)
+        push(block.at[slot], ren_ref.at[sec], 6, swap_sem.at[step_of(0, dy), core], target)
 
     def half_rows(d):
         return pl.ds(d * 128, 128)
@@ -370,21 +375,21 @@
     def ship_far():
         for j in range(2):
             for d, step in steps:
-                push(block.at[j, half_rows(d)], relay.at[d, j], 6, relay_sem.at[d, j], turn(y, step) * 2 + core)
+                push(block.at[j, half_rows(d)], relay.at[d, j], 6, relay_sem.at[d, j], step_of(y, step) * 2 + core)
 
     def relay_far():
         for j in range(2):
             for d, step in steps:
                 arrived(relay.at[d, j], relay_sem.at[d, j])
-                sender = turn(y, 4 - step) * 2 + core
-                push(relay.at[d, j], ren_ref.at[sender, half_rows(d)], 7, far_sem.at[d, core], turn(y, step) * 2 + j)
+                sender = step_of(y, 4 - step) * 2 + core
+                push(relay.at[d, j], ren_ref.at[sender, half_rows(d)], 7, far_sem.at[d, core], step_of(y, step) * 2 + lax.rem(j + core, 2))
 
     def swapped(dy, sender_core):
         sender = turn(y, 4 - dy) * 2 + sender_core
         arrived(ren_ref.at[sender], swap_sem.at[dy, sender_core])
 
-    far = [turn(y, 2) * 2 + j for j in range(2)]
-    near = [[turn(y, dy) * 2 + j for dy in (1, 3)] for j in range(2)]
+    far = [turn(y, 2) * 2 + lax.rem(j + core, 2) for j in range(2)]
+    near = [[step_of(y, dy) * 2 + lax.rem(j + core, 2) for dy in (1, 3)] for j in range(2)]
     here = [2 * y + j for j in range(2)]
 
     sigma_chunk(0)

time: 54.7 us -> 54 us (0.987)
  Pallas kernels: 53.9 us -> 53.3 us
    pallas_call x1, Pallas kernels: 51.5 us -> 50.8 us  [body(): pl.pallas_call(with_totals, out_shape=(jax.ShapeDtypeStruct((256, 256), F...]
where the time goes in v6:
time: 54 us; the launch traced here: 53.9 us
  Pallas kernels  53.3 us (99%)
  between operations  0.64 us (1%)
    pallas_call x1, Pallas kernels, body(): pl.pallas_call(with_totals, out_shape=(jax.ShapeDtypeStruct((256, 256), F...  50.8 us
    pallas_call x1, Pallas kernels, body(): pl.pallas_call(finish, out_shape=(jax.ShapeDtypeStruct((256, 256), BF16),...  2.42 us

profile of v6, /device:TPU:0, one launch (start us, length us, event | category | flops | bytes accessed | tf_op | source)
XLA Modules:
  0.0 53.9 jit_solution(6798709201421183696)
XLA Ops:
  0.6 50.8 %dmrg_step.1 = (f32[256,256]{1,0:T(8,128)}, bf16[8,256,256]{2,1,0:T(8,128)(2,1)}) custom-call(bf16[256,256]{1,0:T(8,128)(2,1)} %bitcast.6, bf16[8,32,128,128]{3,2,1,0:T(8,128)(2,1)} %refs_1_.1, bf16[8,256,256]{2,1,0:T(8,128)(2,1)} %bitcast.5, s32[8,32]{1,0:T(8,128)} %refs_3_.1, s32[8,32]{1,0:T(8,128)} %refs_4_.1), custom_call_target="tpu_custom_call" | custom-call | flops 12999999488 | bytes 12582912 | tf_op jit(solution)/shard_map/dmrg_step/pallas_call | solution.py:470
  51.5 2.4 %finish.1 = (bf16[256,256]{1,0:T(8,128)(2,1)}, f32[8,256,256]{2,1,0:T(8,128)}) custom-call(f32[256,256]{1,0:T(8,128)} %get-tuple-element.6.sig_ref, bf16[8,256,256]{2,1,0:T(8,128)(2,1)} %get-tuple-element.7.ren_ref), custom_call_target="tpu_custom_call" | custom-call | tf_op jit(solution)/shard_map/finish/pallas_call | solution.py:511

commit v7 on v5

--- a/solution.py
+++ b/solution.py
@@ -23,8 +23,8 @@
     psi_ref, left_ref, right_ref, src_hbm, cpl_hbm,
     sig_out, ren_ref,
     src_ref, cpl_ref, sig_ref, left, scaled, right, got, full, full_t, image, zed, parts, block,
-    hop1, hop2, kept, hop3, hop4, relay,
-    load_sem, send_sem, gather_sem, sum_sem, swap_sem, relay_sem, far_sem, own_sem, leave_sem,
+    hop1, hop2, kept, hop3, hop4,
+    load_sem, send_sem, gather_sem, sum_sem, swap_sem, own_sem, leave_sem,
     *totals,
 ):
     acc = (totals[:8], totals[8:])
@@ -364,21 +364,6 @@
     def ship(slot, dy, target):
         push(block.at[slot], ren_ref.at[sec], 6, swap_sem.at[dy, core], target)
 
-    def half_rows(d):
-        return pl.ds(d * 128, 128)
-
-    def ship_far():
-        for j in range(2):
-            for d, step in steps:
-                push(block.at[j, half_rows(d)], relay.at[d, j], 6, relay_sem.at[d, j], turn(y, step) * 2 + core)
-
-    def relay_far():
-        for j in range(2):
-            for d, step in steps:
-                arrived(relay.at[d, j], relay_sem.at[d, j])
-                sender = turn(y, 4 - step) * 2 + core
-                push(relay.at[d, j], ren_ref.at[sender, half_rows(d)], 7, far_sem.at[d, core], turn(y, step) * 2 + j)
-
     def swapped(dy, sender_core):
         sender = turn(y, 4 - dy) * 2 + sender_core
         arrived(ren_ref.at[sender], swap_sem.at[dy, sender_core])
@@ -389,50 +374,47 @@
 
     sigma_chunk(0)
     sum1(0)
-    mix(far, turning=True)
-    renorm(0)
-    ship_far()
-    sum2(0)
     sigma_chunk(1)
     sum1(1)
+    mix(far, turning=True)
+    sum2(0)
+    renorm(0)
+    sum2(1)
+    ship(0, 2, far[0])
+    ship(1, 2, far[1])
     sigma_chunk(2)
     sum1(2)
     sum3(0)
     mix(near[0])
-    relay_far()
-    sum2(1)
+    sum3(1)
     renorm(2)
+    sum2(2)
+    sum4(0)
     ship(2, 1, near[0][0])
     ship(3, 3, near[0][1])
-    sum2(2)
-    sum4(0)
     mix(near[1])
+    sum4(1)
     renorm(4)
+    sum3(2)
+    sum5(0)
     ship(4, 1, near[1][0])
     ship(5, 3, near[1][1])
-    sum3(1)
-    sum5(0)
     mix(here)
-    sum3(2)
-    sum4(1)
+    sum4(2)
+    sum5(1)
     renorm(6)
     ship(7 - core, 0, 2 * y + 1 - core)
     own = pltpu.make_async_copy(block.at[6 + core], ren_ref.at[sec], own_sem)
     own.start()
-    sum4(2)
-    sum5(1)
     sum5(2)
-    for dy in (1, 3):
+    for dy in (2, 1, 3):
         for c in range(2):
             swapped(dy, c)
-    for c in range(2):
-        for d in range(2):
-            arrived(ren_ref.at[turn(y, 2) * 2 + c, half_rows(d)], far_sem.at[d, c])
     swapped(0, 1 - core)
     own.wait()
     for copy in leaves:
         copy.wait()
-    all_sent = (got.at[0, pl.ds(0, 15)], got.at[1, pl.ds(0, 15)], hop1, hop2, hop3, hop4, block.at[pl.ds(0, 7)], relay)
+    all_sent = (got.at[0, pl.ds(0, 15)], got.at[1, pl.ds(0, 15)], hop1, hop2, hop3, hop4, block.at[pl.ds(0, 7)])
     for kind, ref in enumerate(all_sent):
         pltpu.make_async_copy(ref, ref, send_sem.at[kind]).wait()
 
@@ -486,14 +468,11 @@
             vm((2, 4, 256, 128), BF16),
             vm((2, 2, 128, 128), BF16),
             vm((2, 2, 256, 128), BF16),
-            vm((2, 2, 128, 256), BF16),
             pltpu.SemaphoreType.DMA((13,)),
-            pltpu.SemaphoreType.DMA((8,)),
+            pltpu.SemaphoreType.DMA((7,)),
             pltpu.SemaphoreType.DMA((2, 16, 2)),
             pltpu.SemaphoreType.DMA((4, 2, 2, CHUNKS)),
             pltpu.SemaphoreType.DMA((4, 2)),
-            pltpu.SemaphoreType.DMA((2, 2)),
-            pltpu.SemaphoreType.DMA((2, 2)),
             pltpu.SemaphoreType.DMA,
             pltpu.SemaphoreType.DMA((CHUNKS,)),
         ],

time: 54.7 us -> 53.4 us (0.976)
  Pallas kernels: 53.9 us -> 52.5 us
    pallas_call x1, Pallas kernels: 51.5 us -> 50.1 us  [body(): pl.pallas_call(with_totals, out_shape=(jax.ShapeDtypeStruct((256, 256), F...]
where the time goes in v7:
time: 53.4 us; the launch traced here: 53.2 us
  Pallas kernels  52.5 us (98%)
  between operations  0.64 us (1%)
    pallas_call x1, Pallas kernels, body(): pl.pallas_call(with_totals, out_shape=(jax.ShapeDtypeStruct((256, 256), F...  50.1 us
    pallas_call x1, Pallas kernels, body(): pl.pallas_call(finish, out_shape=(jax.ShapeDtypeStruct((256, 256), BF16),...  2.42 us

profile of v7, /device:TPU:0, one launch (start us, length us, event | category | flops | bytes accessed | tf_op | source)
XLA Modules:
  0.0 53.2 jit_solution(943871369385842765)
XLA Ops:
  0.6 50.1 %dmrg_step.1 = (f32[256,256]{1,0:T(8,128)}, bf16[8,256,256]{2,1,0:T(8,128)(2,1)}) custom-call(bf16[256,256]{1,0:T(8,128)(2,1)} %bitcast.6, bf16[8,32,128,128]{3,2,1,0:T(8,128)(2,1)} %refs_1_.1, bf16[8,256,256]{2,1,0:T(8,128)(2,1)} %bitcast.5, s32[8,32]{1,0:T(8,128)} %refs_3_.1, s32[8,32]{1,0:T(8,128)} %refs_4_.1), custom_call_target="tpu_custom_call" | custom-call | flops 12999999488 | bytes 12582912 | tf_op jit(solution)/shard_map/dmrg_step/pallas_call | solution.py:447
  50.7 2.4 %finish.1 = (bf16[256,256]{1,0:T(8,128)(2,1)}, f32[8,256,256]{2,1,0:T(8,128)}) custom-call(f32[256,256]{1,0:T(8,128)} %get-tuple-element.6.sig_ref, bf16[8,256,256]{2,1,0:T(8,128)(2,1)} %get-tuple-element.7.ren_ref), custom_call_target="tpu_custom_call" | custom-call | tf_op jit(solution)/shard_map/finish/pallas_call | solution.py:485

commit v8 on v7

--- a/solution.py
+++ b/solution.py
@@ -23,7 +23,7 @@
     psi_ref, left_ref, right_ref, src_hbm, cpl_hbm,
     sig_out, ren_ref,
     src_ref, cpl_ref, sig_ref, left, scaled, right, got, full, full_t, image, zed, parts, block,
-    hop1, hop2, kept, hop3, hop4,
+    hop1, hop2, kept, hop3,
     load_sem, send_sem, gather_sem, sum_sem, swap_sem, own_sem, leave_sem,
     *totals,
 ):
@@ -35,6 +35,7 @@
 
     barrier = pltpu.get_barrier_semaphore()
     peers = [(z * 4 + turn(x, 1), sec), (z * 4 + turn(x, 3), sec), (turn(z, 1) * 4 + x, sec), (turn(z, 3) * 4 + x, sec)]
+    peers += [(z * 4 + turn(x, 2), sec), (turn(z, 2) * 4 + x, sec)]
     peers += [(op, lax.rem(sec + i, 8)) for i in range(1, 8)]
     for peer in peers:
         pl.semaphore_signal(barrier, inc=1, device_id=peer, device_id_type=MESH)
@@ -82,7 +83,7 @@
 
     for h in range(2):
         loads[h].wait()
-        for sp in (1, -1):
+        for sp in (1, -1, 2):
             pass_on(h, 0, 0, None, sp, 0)
     for h in range(2):
         for sq in (1, -1):
@@ -156,17 +157,10 @@
     both_ways = ((3, 0, 1), (1, 1, -1))
 
     def from_p(h):
-        for dp, half, sp in both_ways:
+        for dp in (3, 1, 2):
             await_piece(h, dp, 0, None)
-            pass_on(h, dp, 0, half, sp, 0)
             for sq in (1, -1):
                 pass_on(h, dp, 0, None, 0, sq)
-
-    def from_p2(h):
-        for half in range(2):
-            await_piece(h, 2, 0, half)
-        for sq in (1, -1):
-            pass_on(h, 2, 0, None, 0, sq)
 
     def from_q(h, dp):
         for dq, half, sq in both_ways:
@@ -187,14 +181,12 @@
     from_q(1, 0)
     loads[2].wait()
     unit_image(0, 0, 0)
+    unit_image(0, 0, 1)
     unit_image(1, 0, 0)
-    from_p2(0)
-    from_p2(1)
-    unit_image(0, 0, 1)
+    scale(2)
     from_q2(0, 0)
     from_q2(1, 0)
     unit_image(1, 0, 1)
-    scale(2)
     from_q(0, 3)
     from_q(1, 3)
     scale(3)
@@ -202,10 +194,10 @@
     from_q(1, 1)
     unit_image(0, 3, 0)
     unit_image(1, 3, 0)
+    from_q(0, 2)
+    from_q(1, 2)
     unit_image(0, 1, 0)
     unit_image(1, 1, 0)
-    from_q(0, 2)
-    from_q(1, 2)
     unit_image(0, 3, 1)
     unit_image(0, 1, 1)
     unit_image(1, 2, 0)
@@ -289,23 +281,10 @@
             total = parts[h, q, :, rows, :].astype(F32)
             total = total + hop2[h, 0, :, rows, :].astype(F32) + hop2[h, 1, :, rows, :].astype(F32)
             kept[h, :, rows, :] = total.astype(BF16)
-            for d, step in steps:
+            for i, step in enumerate((1, 3, 2)):
                 start(
-                    kept.at[h, turn(p, 2), half_of(c, d), :], hop3.at[h, d, small(c), :],
-                    4, sum_sem.at[2, h, d, c], at(h, step, 0),
-                )
-
-    def sum4(c):
-        for h in range(2):
-            p, q = coords[h]
-            for d, step in steps:
-                arrived(hop3.at[h, d, small(c), :], sum_sem.at[2, h, d, c])
-                near = turn(p, step)
-                old = kept[h, near, half_of(c, d), :].astype(F32)
-                kept[h, near, half_of(c, d), :] = (old + hop3[h, d, small(c), :].astype(F32)).astype(BF16)
-                start(
-                    kept.at[h, near, all_rows(c), :], hop4.at[h, d, all_rows(c), :],
-                    5, sum_sem.at[3, h, d, c], at(h, step, 0),
+                    kept.at[h, turn(p, step), rows, :], hop3.at[h, i, rows, :],
+                    4, sum_sem.at[2, h, i, c], at(h, step, 0),
                 )
 
     leaves = []
@@ -314,9 +293,10 @@
         rows = all_rows(c)
         for h in range(2):
             p, q = coords[h]
-            for d, step in steps:
-                arrived(hop4.at[h, d, rows, :], sum_sem.at[3, h, d, c])
-            total = kept[h, p, rows, :].astype(F32) + hop4[h, 0, rows, :].astype(F32) + hop4[h, 1, rows, :].astype(F32)
+            total = kept[h, p, rows, :].astype(F32)
+            for i in range(3):
+                arrived(hop3.at[h, i, rows, :], sum_sem.at[2, h, i, c])
+                total = total + hop3[h, i, rows, :].astype(F32)
             sig_ref[rows, pl.ds(h * 128, 128)] = total * (128 ** -0.5)
         leaves.append(pltpu.make_async_copy(sig_ref.at[rows, :], sig_out.at[rows, :], leave_sem.at[c]))
         leaves[-1].start()
@@ -362,7 +342,7 @@
         ).start()
 
     def ship(slot, dy, target):
-        push(block.at[slot], ren_ref.at[sec], 6, swap_sem.at[dy, core], target)
+        push(block.at[slot], ren_ref.at[sec], 5, swap_sem.at[dy, core], target)
 
     def swapped(dy, sender_core):
         sender = turn(y, 4 - dy) * 2 + sender_core
@@ -389,18 +369,15 @@
     sum3(1)
     renorm(2)
     sum2(2)
-    sum4(0)
     ship(2, 1, near[0][0])
     ship(3, 3, near[0][1])
     mix(near[1])
-    sum4(1)
+    sum5(0)
     renorm(4)
     sum3(2)
-    sum5(0)
     ship(4, 1, near[1][0])
     ship(5, 3, near[1][1])
     mix(here)
-    sum4(2)
     sum5(1)
     renorm(6)
     ship(7 - core, 0, 2 * y + 1 - core)
@@ -414,7 +391,7 @@
     own.wait()
     for copy in leaves:
         copy.wait()
-    all_sent = (got.at[0, pl.ds(0, 15)], got.at[1, pl.ds(0, 15)], hop1, hop2, hop3, hop4, block.at[pl.ds(0, 7)])
+    all_sent = (got.at[0, pl.ds(0, 15)], got.at[1, pl.ds(0, 15)], hop1, hop2, hop3, block.at[pl.ds(0, 7)])
     for kind, ref in enumerate(all_sent):
         pltpu.make_async_copy(ref, ref, send_sem.at[kind]).wait()
 
@@ -466,12 +443,11 @@
             vm((2, 2, 4, 128, 128), BF16),
             vm((2, 2, 4, 256, 128), BF16),
             vm((2, 4, 256, 128), BF16),
-            vm((2, 2, 128, 128), BF16),
-            vm((2, 2, 256, 128), BF16),
+            vm((2, 3, 256, 128), BF16),
             pltpu.SemaphoreType.DMA((13,)),
-            pltpu.SemaphoreType.DMA((7,)),
+            pltpu.SemaphoreType.DMA((6,)),
             pltpu.SemaphoreType.DMA((2, 16, 2)),
-            pltpu.SemaphoreType.DMA((4, 2, 2, CHUNKS)),
+            pltpu.SemaphoreType.DMA((3, 2, 3, CHUNKS)),
             pltpu.SemaphoreType.DMA((4, 2)),
             pltpu.SemaphoreType.DMA,
             pltpu.SemaphoreType.DMA((CHUNKS,)),

time: 53.4 us -> 52.9 us (level)
  the two profiles are of different devices: /device:TPU:0 before, /device:TPU:1 now
where the time goes in v8:
time: 52.9 us; the launch traced here: 52.8 us
  Pallas kernels  52.2 us (99%)
  between operations  0.64 us (1%)
    pallas_call x1, Pallas kernels, body(): pl.pallas_call(with_totals, out_shape=(jax.ShapeDtypeStruct((256, 256), F...  49.8 us
    pallas_call x1, Pallas kernels, body(): pl.pallas_call(finish, out_shape=(jax.ShapeDtypeStruct((256, 256), BF16),...  2.42 us

profile of v8, /device:TPU:1, one launch (start us, length us, event | category | flops | bytes accessed | tf_op | source)
XLA Modules:
  0.0 52.8 jit_solution(11424191685957622581)
XLA Ops:
  0.6 49.8 %dmrg_step.1 = (f32[256,256]{1,0:T(8,128)}, bf16[8,256,256]{2,1,0:T(8,128)(2,1)}) custom-call(bf16[256,256]{1,0:T(8,128)(2,1)} %bitcast.6, bf16[8,32,128,128]{3,2,1,0:T(8,128)(2,1)} %refs_1_.1, bf16[8,256,256]{2,1,0:T(8,128)(2,1)} %bitcast.5, s32[8,32]{1,0:T(8,128)} %refs_3_.1, s32[8,32]{1,0:T(8,128)} %refs_4_.1), custom_call_target="tpu_custom_call" | custom-call | flops 12999999488 | bytes 12582912 | tf_op jit(solution)/shard_map/dmrg_step/pallas_call | solution.py:424
  50.4 2.4 %finish.1 = (bf16[256,256]{1,0:T(8,128)(2,1)}, f32[8,256,256]{2,1,0:T(8,128)}) custom-call(f32[256,256]{1,0:T(8,128)} %get-tuple-element.6.sig_ref, bf16[8,256,256]{2,1,0:T(8,128)(2,1)} %get-tuple-element.7.ren_ref), custom_call_target="tpu_custom_call" | custom-call | tf_op jit(solution)/shard_map/finish/pallas_call | solution.py:461

commit v9 on v8

--- a/solution.py
+++ b/solution.py
@@ -95,7 +95,7 @@
 
         @pl.loop(2 * part, 2 * part + 2)
         def _(k):
-            @pl.loop(0, 32, unroll=8)
+            @pl.loop(0, 32, unroll=4)
             def _(s):
                 level = cpl_ref[k, s]
                 coef = jnp.where(
@@ -122,13 +122,10 @@
                 issue(t + 1, u + 1)
             drain(t, u)
 
-    waiting = []
-
     def unit_image(h, dz, other):
         j = x // 2
-        if other:
-            j = 1 - j
-        zz = turn(z, dz)
+        j = j + other * (1 - 2 * j)
+        zz = lax.rem(z + dz, 4)
         o, to = zz * 4 + 2 * j, pl.ds(pl.multiple_of(zz * 32 + j * 16, 16), 16)
 
         def put(ref, first, second, at_sector):
@@ -136,23 +133,30 @@
                 two = jnp.concatenate([first[s * 8 : s * 8 + 8], second[s * 8 : s * 8 + 8]], axis=0)
                 ref[h * 16 + at_sector + s, to, :] = two.astype(BF16)
 
+        def issue(u):
+            for unit in range(2):
+                pltpu.matmul_push_rhs(right[2 * u + unit], u % 2, unit)
+                for n in range(2):
+                    feed(unit, 4 * (u % 2) + 2 * n, got[h, o + n], u % 2 if n == 0 else None)
+
         def drain(u):
-            if u == 0:
-                put(full, got[h, o, :64].astype(F32), got[h, o + 1, :64].astype(F32), 0)
-                put(full, got[h, o, 64:].astype(F32), got[h, o + 1, 64:].astype(F32), 8)
             for unit in range(2):
                 mine = acc[unit][4 * (u % 2) : 4 * (u % 2) + 4]
                 for n in range(2):
                     put(image.at[2 * u + unit], pltpu.matmul_pop(mine[n]), pltpu.matmul_pop(mine[2 + n]), 8 * n)
 
-        for u in range(4):
-            for unit in range(2):
-                pltpu.matmul_push_rhs(right[2 * u + unit], u % 2, unit)
-                for n in range(2):
-                    feed(unit, 4 * (u % 2) + 2 * n, got[h, o + n], u % 2 if n == 0 else None)
-            if waiting:
-                waiting.pop()()
-            waiting.append(functools.partial(drain, u))
+        issue(0)
+        put(full, got[h, o, :64].astype(F32), got[h, o + 1, :64].astype(F32), 0)
+        put(full, got[h, o, 64:].astype(F32), got[h, o + 1, 64:].astype(F32), 8)
+        for u in range(1, 4):
+            issue(u)
+            drain(u - 1)
+        drain(3)
+
+    def unit_images(count, which):
+        @pl.loop(0, count)
+        def _(i):
+            unit_image(*which(i))
 
     both_ways = ((3, 0, 1), (1, 1, -1))
 
@@ -180,39 +184,28 @@
     from_q(0, 0)
     from_q(1, 0)
     loads[2].wait()
-    unit_image(0, 0, 0)
-    unit_image(0, 0, 1)
-    unit_image(1, 0, 0)
+    unit_images(3, lambda i: (i // 2, 0, lax.rem(i, 2)))
     scale(2)
     from_q2(0, 0)
     from_q2(1, 0)
-    unit_image(1, 0, 1)
+    unit_images(1, lambda i: (1, 0, 1))
     from_q(0, 3)
     from_q(1, 3)
     scale(3)
     from_q(0, 1)
     from_q(1, 1)
-    unit_image(0, 3, 0)
-    unit_image(1, 3, 0)
+    unit_images(2, lambda i: (i, 3, 0))
     from_q(0, 2)
     from_q(1, 2)
-    unit_image(0, 1, 0)
-    unit_image(1, 1, 0)
-    unit_image(0, 3, 1)
-    unit_image(0, 1, 1)
-    unit_image(1, 2, 0)
-    from_q2(0, 3)
-    from_q2(0, 1)
-    unit_image(0, 2, 0)
-    from_q2(1, 3)
-    unit_image(1, 3, 1)
-    from_q2(1, 1)
-    unit_image(1, 1, 1)
+    unit_images(2, lambda i: (i, 1, 0))
+    unit_images(3, lambda i: (i // 2, 3 + 2 * i + 3 * (i // 2), 1 - i // 2))
+    for h in (1, 0):
+        from_q2(h, 3)
+        from_q2(h, 1)
+    unit_images(3, lambda i: (1 - i // 2, 3 + 2 * i + 3 * (i // 2), 1 - i // 2))
     from_q2(0, 2)
-    unit_image(0, 2, 1)
     from_q2(1, 2)
-    unit_image(1, 2, 1)
-    waiting.pop()()
+    unit_images(2, lambda i: (i, 2, 1))
 
     def source(k, s):
         return lax.rem(src_ref[k, s], 32)
@@ -321,15 +314,15 @@
                 for n in range(4):
                     zed[j, t, n * 64 : n * 64 + 64, :] = pltpu.matmul_pop(acc[j][4 * (u % 2) + n]).astype(BF16)
 
-        in_turns(16, issue, drain, 4)
+        in_turns(16, issue, drain, 2)
 
     def renorm(slot):
-        @pl.loop(0, 2)
+        @pl.loop(0, 4)
         def _(i):
-            for e in range(8):
+            for e in range(4):
                 for j in range(2):
-                    pltpu.matmul_push_rhs(zed[j, 8 * i + e], e % 2, j)
-                    feed(j, 0, full_t[8 * i + e], e % 2)
+                    pltpu.matmul_push_rhs(zed[j, 4 * i + e], e % 2, j)
+                    feed(j, 0, full_t[4 * i + e], e % 2)
 
         for j in range(2):
             for n in range(4):

time: 52.9 us -> 54.3 us (1.026)
  Pallas kernels: 52.2 us -> 53.5 us
    pallas_call x1, Pallas kernels: 49.8 us -> 51.1 us  [body(): pl.pallas_call(with_totals, out_shape=(jax.ShapeDtypeStruct((256, 256), F...]
where the time goes in v9:
time: 54.3 us; the launch traced here: 54.1 us
  Pallas kernels  53.5 us (99%)
  between operations  0.64 us (1%)
    pallas_call x1, Pallas kernels, body(): pl.pallas_call(with_totals, out_shape=(jax.ShapeDtypeStruct((256, 256), F...  51.1 us
    pallas_call x1, Pallas kernels, body(): pl.pallas_call(finish, out_shape=(jax.ShapeDtypeStruct((256, 256), BF16),...  2.42 us

profile of v9, /device:TPU:1, one launch (start us, length us, event | category | flops | bytes accessed | tf_op | source)
XLA Modules:
  0.0 54.1 jit_solution(387585680627673216)
XLA Ops:
  0.6 51.1 %dmrg_step.1 = (f32[256,256]{1,0:T(8,128)}, bf16[8,256,256]{2,1,0:T(8,128)(2,1)}) custom-call(bf16[256,256]{1,0:T(8,128)(2,1)} %bitcast.6, bf16[8,32,128,128]{3,2,1,0:T(8,128)(2,1)} %refs_1_.1, bf16[8,256,256]{2,1,0:T(8,128)(2,1)} %bitcast.5, s32[8,32]{1,0:T(8,128)} %refs_3_.1, s32[8,32]{1,0:T(8,128)} %refs_4_.1), custom_call_target="tpu_custom_call" | custom-call | flops 12999999488 | bytes 12582912 | tf_op jit(solution)/shard_map/dmrg_step/pallas_call | solution.py:417
  51.7 2.4 %finish.1 = (bf16[256,256]{1,0:T(8,128)(2,1)}, f32[8,256,256]{2,1,0:T(8,128)}) custom-call(f32[256,256]{1,0:T(8,128)} %get-tuple-element.6.sig_ref, bf16[8,256,256]{2,1,0:T(8,128)(2,1)} %get-tuple-element.7.ren_ref), custom_call_target="tpu_custom_call" | custom-call | tf_op jit(solution)/shard_map/finish/pallas_call | solution.py:454

commit v10 on v8

--- a/solution.py
+++ b/solution.py
@@ -11,7 +11,7 @@
 MESH = pl.DeviceIdType.MESH
 F32 = jnp.float32
 BF16 = jnp.bfloat16
-CUTS = (0, 8, 20, 32)
+CUTS = (0, 8, 24, 32)
 CHUNKS = len(CUTS) - 1
 
 
@@ -229,6 +229,10 @@
 
         def drain(t, u):
             rows = pl.ds(pl.multiple_of(CUTS[c] * 8 + t * 16, 16), 16)
+            if c < 2:
+                turned = CUTS[c] // 2 + t
+                for n in range(2):
+                    full_t[turned, :, n * 128 : n * 128 + 128] = full[2 * turned + n].T
             for n in range(2):
                 first, second = pltpu.matmul_pop(acc[0][2 * (u % 2) + n]), pltpu.matmul_pop(acc[1][2 * (u % 2) + n])
                 for o in range(8):
@@ -315,8 +319,10 @@
 
         def drain(t, u):
             if turning:
-                for n in range(2):
-                    full_t[t, :, n * 128 : n * 128 + 128] = full[2 * t + n].T
+                turned, n, m = CUTS[2] // 2 + t // 4, u % 2, u // 2
+                full_t[turned, m * 128 : m * 128 + 128, n * 128 : n * 128 + 128] = full[
+                    2 * turned + n, :, m * 128 : m * 128 + 128
+                ].T
             for j in range(2):
                 for n in range(4):
                     zed[j, t, n * 64 : n * 64 + 64, :] = pltpu.matmul_pop(acc[j][4 * (u % 2) + n]).astype(BF16)
@@ -359,30 +365,30 @@
     mix(far, turning=True)
     sum2(0)
     renorm(0)
-    sum2(1)
     ship(0, 2, far[0])
     ship(1, 2, far[1])
     sigma_chunk(2)
     sum1(2)
+    sum2(1)
+    mix(near[0])
     sum3(0)
-    mix(near[0])
-    sum3(1)
     renorm(2)
-    sum2(2)
     ship(2, 1, near[0][0])
     ship(3, 3, near[0][1])
+    sum2(2)
     mix(near[1])
-    sum5(0)
     renorm(4)
-    sum3(2)
     ship(4, 1, near[1][0])
     ship(5, 3, near[1][1])
+    sum3(1)
     mix(here)
-    sum5(1)
+    sum3(2)
+    sum5(0)
     renorm(6)
     ship(7 - core, 0, 2 * y + 1 - core)
     own = pltpu.make_async_copy(block.at[6 + core], ren_ref.at[sec], own_sem)
     own.start()
+    sum5(1)
     sum5(2)
     for dy in (2, 1, 3):
         for c in range(2):

time: 52.9 us -> 49.9 us (0.943)
  the two profiles are of different devices: /device:TPU:1 before, /device:TPU:0 now
where the time goes in v10:
time: 49.9 us; the launch traced here: 49.8 us
  Pallas kernels  49.1 us (98%)
  between operations  0.64 us (1%)
    pallas_call x1, Pallas kernels, body(): pl.pallas_call(with_totals, out_shape=(jax.ShapeDtypeStruct((256, 256), F...  46.7 us
    pallas_call x1, Pallas kernels, body(): pl.pallas_call(finish, out_shape=(jax.ShapeDtypeStruct((256, 256), BF16),...  2.42 us

profile of v10, /device:TPU:0, one launch (start us, length us, event | category | flops | bytes accessed | tf_op | source)
XLA Modules:
  0.0 49.8 jit_solution(8499902342285247150)
XLA Ops:
  0.6 46.7 %dmrg_step.1 = (f32[256,256]{1,0:T(8,128)}, bf16[8,256,256]{2,1,0:T(8,128)(2,1)}) custom-call(bf16[256,256]{1,0:T(8,128)(2,1)} %bitcast.6, bf16[8,32,128,128]{3,2,1,0:T(8,128)(2,1)} %refs_1_.1, bf16[8,256,256]{2,1,0:T(8,128)(2,1)} %bitcast.5, s32[8,32]{1,0:T(8,128)} %refs_3_.1, s32[8,32]{1,0:T(8,128)} %refs_4_.1), custom_call_target="tpu_custom_call" | custom-call | flops 12999999488 | bytes 12582912 | tf_op jit(solution)/shard_map/dmrg_step/pallas_call | solution.py:430
  47.4 2.4 %finish.1 = (bf16[256,256]{1,0:T(8,128)(2,1)}, f32[8,256,256]{2,1,0:T(8,128)}) custom-call(f32[256,256]{1,0:T(8,128)} %get-tuple-element.6.sig_ref, bf16[8,256,256]{2,1,0:T(8,128)(2,1)} %get-tuple-element.7.ren_ref), custom_call_target="tpu_custom_call" | custom-call | tf_op jit(solution)/shard_map/finish/pallas_call | solution.py:467

commit v11 on v10

--- a/solution.py
+++ b/solution.py
@@ -373,22 +373,22 @@
     mix(near[0])
     sum3(0)
     renorm(2)
+    sum2(2)
     ship(2, 1, near[0][0])
     ship(3, 3, near[0][1])
-    sum2(2)
     mix(near[1])
+    sum3(1)
     renorm(4)
     ship(4, 1, near[1][0])
     ship(5, 3, near[1][1])
-    sum3(1)
+    sum5(0)
     mix(here)
     sum3(2)
-    sum5(0)
+    sum5(1)
     renorm(6)
     ship(7 - core, 0, 2 * y + 1 - core)
     own = pltpu.make_async_copy(block.at[6 + core], ren_ref.at[sec], own_sem)
     own.start()
-    sum5(1)
     sum5(2)
     for dy in (2, 1, 3):
         for c in range(2):

time: 49.9 us -> 50.9 us (1.020)
  Pallas kernels: 49.1 us -> 49.9 us
    pallas_call x1, Pallas kernels: 46.7 us -> 47.5 us  [body(): pl.pallas_call(with_totals, out_shape=(jax.ShapeDtypeStruct((256, 256), F...]
where the time goes in v11:
time: 50.9 us; the launch traced here: 50.5 us
  Pallas kernels  49.9 us (98%)
  between operations  0.64 us (1%)
    pallas_call x1, Pallas kernels, body(): pl.pallas_call(with_totals, out_shape=(jax.ShapeDtypeStruct((256, 256), F...  47.5 us
    pallas_call x1, Pallas kernels, body(): pl.pallas_call(finish, out_shape=(jax.ShapeDtypeStruct((256, 256), BF16),...  2.42 us

profile of v11, /device:TPU:0, one launch (start us, length us, event | category | flops | bytes accessed | tf_op | source)
XLA Modules:
  0.0 50.5 jit_solution(986508973595937196)
XLA Ops:
  0.6 47.5 %dmrg_step.1 = (f32[256,256]{1,0:T(8,128)}, bf16[8,256,256]{2,1,0:T(8,128)(2,1)}) custom-call(bf16[256,256]{1,0:T(8,128)(2,1)} %bitcast.6, bf16[8,32,128,128]{3,2,1,0:T(8,128)(2,1)} %refs_1_.1, bf16[8,256,256]{2,1,0:T(8,128)(2,1)} %bitcast.5, s32[8,32]{1,0:T(8,128)} %refs_3_.1, s32[8,32]{1,0:T(8,128)} %refs_4_.1), custom_call_target="tpu_custom_call" | custom-call | flops 12999999488 | bytes 12582912 | tf_op jit(solution)/shard_map/dmrg_step/pallas_call | solution.py:430
  48.1 2.4 %finish.1 = (bf16[256,256]{1,0:T(8,128)(2,1)}, f32[8,256,256]{2,1,0:T(8,128)}) custom-call(f32[256,256]{1,0:T(8,128)} %get-tuple-element.6.sig_ref, bf16[8,256,256]{2,1,0:T(8,128)(2,1)} %get-tuple-element.7.ren_ref), custom_call_target="tpu_custom_call" | custom-call | tf_op jit(solution)/shard_map/finish/pallas_call | solution.py:467
